TPU v7x, 512 devices: a whole 4x4x16 slice. The times are simulated.
512 devices in a mesh: corpus: 16 (over z), frow: 4 (over x), fcol: 8 (over y, core).
Axes of the slice: x: 4, y: 4, z: 16, core: 2. Of those that a mesh axis runs over, the one named last changes fastest.
Arguments:
- feature_slab: bfloat16 [32768, 4096], P('corpus', ('frow', 'fcol')), may hold values from -6 to 6
- test_preconditioned: bfloat16 [16384, 4096], P('corpus', ('frow', 'fcol')), may hold values from -0.09375 to 0.09375
- train_weight: float32 [32768], P('corpus'), may hold values from 0.1 to 1
- pair_tests: int32 [16, 16], P('corpus'), may hold values from 0 to 127, as said below
- pair_trains: int32 [16, 16], P('corpus'), may hold values from 0 to 15
- pair_counts: int32 [16], P('corpus'), may hold values from 4 to 16
Outputs:
- gram_upper: float32 [4096, 4, 1024], P(('frow', 'corpus'), None, 'fcol')
- pair_scores: float32 [16, 16, 128, 128], P('corpus', None, ('frow', 'fcol'))
Inputs may be any that keep to these rules, and one draw needn't show every extreme that they name: `pair_tests`: test block g is rows g * 128 to g * 128 + 127 of test_preconditioned, held by corpus index g // 8. Among the first pair_counts[c] slots of row c, at most 2 name blocks held by one corpus index.
All inputs are finite; a program needn't handle non-finite values.
Results may differ from a plain program's by a relative error of at most 0.0003.
Values may be sent and summed in bfloat16 or wider, within the bound.
No kernel may reach another device: no remote copies, remote signals or barrier semaphores. Data moves between devices by JAX's collectives and lax.ppermute only.
A program may use at most 64 MiB of HBM per device.

v0:
```python
import jax
import jax.numpy as jnp
from jax import lax
from jax.sharding import PartitionSpec as P

TB = 128
PAIRS = 16


def shards(feature_slab, test_preconditioned, train_weight, pair_tests, pair_trains, pair_counts):
    slab_rows, feat_width = feature_slab.shape
    row_groups = lax.axis_size("frow")
    col_groups = lax.axis_size("fcol")
    corpus_size = lax.axis_size("corpus")
    frow_at = lax.axis_index("frow")
    fcol_at = lax.axis_index("fcol")
    block_width = feat_width * col_groups
    column_panel = lax.all_gather(feature_slab, "frow", axis=1, tiled=True)
    column_global = (
        jnp.arange(row_groups)[:, None] * block_width
        + fcol_at * feat_width
        + jnp.arange(feat_width)[None, :]
    ).reshape(-1)
    product = lax.dot_general(
        lax.all_gather(feature_slab, "fcol", axis=1, tiled=True),
        column_panel,
        (((0,), (0,)), ((), ())),
        preferred_element_type=jnp.float32,
    )
    row_global = frow_at * block_width + jnp.arange(product.shape[0])
    kernel_tile = jnp.where(row_global[:, None] <= column_global[None, :], product, 0.0)
    summed_tile = lax.psum_scatter(kernel_tile, "corpus", scatter_dimension=0, tiled=True)
    norm_scale = (slab_rows * corpus_size) ** (-0.5)
    gram_upper = (summed_tile * norm_scale).reshape(summed_tile.shape[0], row_groups, feat_width)
    test_ids = pair_tests[0]
    train_ids = pair_trains[0]
    pair_count = pair_counts[0]
    slot_ids = jnp.arange(PAIRS, dtype=jnp.int32)
    is_live = slot_ids < pair_count
    train_blocks = feature_slab.reshape(-1, TB, feat_width)
    chosen = jnp.take(train_blocks, train_ids, axis=0)
    test_piece = lax.all_gather(test_preconditioned, "corpus", axis=0, tiled=True)
    row_index = test_ids[:, None] * TB + jnp.arange(TB)[None, :]
    inside = (row_index >= 0) & (row_index < test_piece.shape[0])
    test_rows = jnp.take(test_piece, jnp.clip(row_index, 0, test_piece.shape[0] - 1), axis=0)
    test_rows = jnp.where(inside[:, :, None], test_rows, jnp.zeros((), test_rows.dtype))
    partial_scores = jnp.einsum(
        "pak,pbk->pab", test_rows, chosen, preferred_element_type=jnp.float32
    )
    summed_scores = lax.psum_scatter(
        partial_scores, ("frow", "fcol"), scatter_dimension=1, tiled=True
    )
    column_weights = jnp.take(train_weight.reshape(-1, TB), train_ids, axis=0)
    pair_scores = (
        summed_scores * column_weights[:, None, :] * is_live.astype(jnp.float32)[:, None, None]
    )
    return (gram_upper, pair_scores[None])


def solution(mesh):
    return jax.shard_map(
        shards,
        mesh=mesh,
        in_specs=(
            P("corpus", ("frow", "fcol")),
            P("corpus", ("frow", "fcol")),
            P("corpus"),
            P("corpus", None),
            P("corpus", None),
            P("corpus"),
        ),
        out_specs=(P(("frow", "corpus"), None, "fcol"), P("corpus", None, ("frow", "fcol"), None)),
        check_vma=False,
    )
```

profile of v0, /device:TPU:2, one launch (start us, length us, event | category | flops | bytes accessed | tf_op | source)
XLA Modules:
  0.0 370.9 jit_solution(16974981919199826959)
XLA Ops:
  7.2 0.7 all-gather.8.cloned.1.call-update
  8.0 0.7 all-gather.6.cloned.1.call-update
  8.7 0.7 all-gather.4.cloned.1.call-update
  9.5 0.7 fusion.17
  10.1 1.7 gather_fusion.1
  11.9 0.1 fusion.16
  12.0 0.1 fusion.10
  12.0 81.3 %all-gather.8.cloned.1.call-done = bf16[16384,128]{1,0:T(8,128)(2,1)} async-done(((bf16[1024,128]{1,0:T(8,128)(2,1)}), bf16[16384,128]{1,0:T(8,128)(2,1)}) %all-gather.8.cloned.1.call-update) | async-done | bytes 4194320 | tf_op jit(solution)/shard_map/all_gather | solution.py:42
  93.4 8.3 %gather_fusion = bf16[2048,128]{1,0:T(8,128)(2,1)S(1)} fusion(bf16[16384,128]{1,0:T(8,128)(2,1)} %all-gather.8.cloned.1.call-done, s32[2048]{0:T(1024)S(1)} %fusion.10), kind=kCustom, calls=%fused_computation | custom fusion | bytes 1056768 | tf_op jit(solution)/shard_map/jit(_take)/gather | solution.py:45
  101.7 2.2 fusion
  103.9 1.6 copy.8
  105.5 0.0 reduce-scatter.3.cloned.1.call-start
  105.6 0.1 add_bitcast_fusion
  105.6 27.8 %all-gather.6.cloned.1.call-done = bf16[2048,512]{1,0:T(8,128)(2,1)} async-done(((bf16[2048,128]{1,0:T(8,128)(2,1)}), bf16[2048,512]{1,0:T(8,128)(2,1)}) %all-gather.6.cloned.1.call-update) | async-done | bytes 2097168 | tf_op jit(solution)/shard_map/all_gather | solution.py:18
  133.5 47.6 %all-gather.4.cloned.1.call-done = bf16[2048,1024]{1,0:T(8,128)(2,1)} async-done(((bf16[2048,128]{1,0:T(8,128)(2,1)}), bf16[2048,1024]{1,0:T(8,128)(2,1)}) %all-gather.4.cloned.1.call-update) | async-done | bytes 4194320 | tf_op jit(solution)/shard_map/all_gather | solution.py:25
  181.1 6.6 %compare_select_fusion = f32[1024,512]{1,0:T(8,128)} fusion(bf16[2048,1024]{1,0:T(8,128)(2,1)} %all-gather.4.cloned.1.call-done, bf16[2048,512]{1,0:T(8,128)(2,1)} %all-gather.6.cloned.1.call-done, s32[512]{0:T(512)S(1)} %add_bitcast_fusion, s32[1024]{0:T(1024)S(1)} %iota_add_fusion.1), kind=kOutput, calls=%fused_computation.3 | convolution fusion | flops 2148532224 | bytes 8394752 | tf_op jit(solution)/shard_map/dot_general | solution.py:24
  188.4 0.6 gather_fusion.2
  188.9 0.1 broadcast_select_fusion
  189.0 97.7 %reduce-scatter.5.cloned.1.call-done = f32[16,4,128]{2,0,1:T(8,128)} async-done(((f32[16,128,128]{2,0,1:T(8,128)}), f32[16,4,128]{2,0,1:T(8,128)}) %reduce-scatter.5.cloned.1.call-update) | async-done | bytes 32784 | tf_op jit(solution)/shard_map/reduce_scatter | solution.py:50
  286.7 0.8 multiply_bitcast_fusion
  287.5 0.6 copy.9
  288.2 74.6 %reduce-scatter.3.cloned.1.call-done = f32[64,512]{1,0:T(8,128)} async-done(((f32[1024,512]{1,0:T(8,128)}), f32[64,512]{1,0:T(8,128)}) %reduce-scatter.3.cloned.1.call-update) | async-done | bytes 131088 | tf_op jit(solution)/shard_map/reduce_scatter | solution.py:32
  362.8 0.9 broadcast_multiply_fusion
  363.7 0.7 reshape.179
  (18 shorter events, 0.2 us)
Async XLA Ops:
  7.2 181.2 %copy-start = (f32[2048]{0:T(1024)S(1)}, f32[2048]{0:T(1024)}, u32[]{:S(2)}) copy-start(f32[2048]{0:T(1024)} %param.8) | copy-start | bytes 24580
  7.2 4.7 %copy-start.1 = (s32[1,16]{1,0:T(1,128)S(1)}, s32[1,16]{1,0:T(1,128)}, u32[]{:S(2)}) copy-start(s32[1,16]{1,0:T(1,128)} %param.10) | copy-start | bytes 196
  7.2 4.7 %copy-start.2 = (s32[1,16]{1,0:T(1,128)S(1)}, s32[1,16]{1,0:T(1,128)}, u32[]{:S(2)}) copy-start(s32[1,16]{1,0:T(1,128)} %param.9) | copy-start | bytes 196
  7.2 86.2 %all-gather.8.cloned.1.call-start = ((), (), s32[]{:S(2)}) async-start(), calls=%async_computation.5 | async-start | bytes 4456448 | tf_op jit(solution)/shard_map/all_gather | solution.py:42
  7.9 125.5 %all-gather.6.cloned.1.call-start = ((), (), s32[]{:S(2)}) async-start(), calls=%async_computation.3 | async-start | bytes 2621440 | tf_op jit(solution)/shard_map/all_gather | solution.py:18
  8.7 172.4 %all-gather.4.cloned.1.call-start = ((), (), s32[]{:S(2)}) async-start(), calls=%async_computation.2 | async-start | bytes 4718592 | tf_op jit(solution)/shard_map/all_gather | solution.py:25
  9.4 277.3 %reduce-scatter.5.cloned.1.call-start = ((), (), s32[]{:S(2)}) async-start(), calls=%async_computation.6 | async-start | bytes 1081344 | tf_op jit(solution)/shard_map/reduce_scatter | solution.py:50
  105.5 257.3 %reduce-scatter.3.cloned.1.call-start = ((), (), s32[]{:S(2)}) async-start(), calls=%async_computation.4 | async-start | bytes 2228224 | tf_op jit(solution)/shard_map/reduce_scatter | solution.py:32
Sparse Core Ops, SparseCore 0:
  10.1 83.2 all-gather.7
  95.5 37.9 all-gather.5
  135.6 45.4 all-gather.3
  185.3 101.3 reduce-scatter.4
  289.6 73.1 reduce-scatter.2
where the time goes:
time: 371 us
  waiting for transfers between devices  331 us (89%)
  between operations  14.5 us (4%)
  local copies, waits for them, and re-layouts  13.5 us (4%)
  matrix products  8.73 us (2%)
    reduce_scatter x1, waiting for transfers between devices, shards(): lax.psum_scatter(partial_scores, ('frow', 'fcol'), scatter_dimension=1, t...  97.7 us
    all_gather x1, waiting for transfers between devices, shards(): lax.all_gather(test_preconditioned, 'corpus', axis=0, tiled=True)  81.3 us
    reduce_scatter x1, waiting for transfers between devices, shards(): lax.psum_scatter(kernel_tile, 'corpus', scatter_dimension=0, tiled=True)  74.6 us
    all_gather x1, waiting for transfers between devices, shards(): lax.all_gather(feature_slab, 'fcol', axis=1, tiled=True)  47.6 us
    all_gather x1, waiting for transfers between devices, shards(): column_panel = lax.all_gather(feature_slab, 'frow', axis=1, tiled=True)  27.8 us
    gather x1, local copies, waits for them, and re-layouts, shards(): jnp.take(test_piece, jnp.clip(row_index, 0, test_piece.shape[0] - 1), axi...  8.3 us
  transfers between devices with their start and end apart: 5, of which 5 were waited for; matrix products, arithmetic and copies ran while one was open for 6% of the time, Pallas kernels for 0%

commit v1 on v0

v1 whole, which is shorter than its diff:
```python
import functools

import jax
import jax.numpy as jnp
from jax import lax
from jax.experimental import pallas as pl
from jax.experimental.pallas import tpu as pltpu
from jax.sharding import PartitionSpec as P

TB = 128
PAIRS = 16
CAP = 2
CORES = 2


def gram_kernel(scale, steps, x_size, y_size, place, *refs):
    column_refs, row_refs = refs[:x_size], refs[x_size:x_size + CORES * y_size]
    out_ref, total = refs[-2:]
    step = pl.program_id(0)
    rows = jnp.concatenate([ref[...] for ref in row_refs], axis=1)
    columns = jnp.concatenate([ref[...] for ref in column_refs], axis=1)
    product = lax.dot_general(
        rows, columns, (((0,), (0,)), ((), ())), preferred_element_type=jnp.float32
    )

    @pl.when(step == 0)
    def _():
        total[...] = product

    @pl.when(step > 0)
    def _():
        total[...] += product

    @pl.when(step == steps - 1)
    def _():
        width = out_ref.shape[1] // x_size
        frow_at, y_at, core_at = place[0], place[1], place[2]
        row_iota = lax.broadcasted_iota(jnp.int32, (width, width), 0)
        column_iota = lax.broadcasted_iota(jnp.int32, (width, width), 1)
        for r in range(CORES * y_size):
            row_y = lax.rem(y_at + r // CORES, y_size)
            row_core = core_at if r % CORES == 0 else CORES - 1 - core_at
            row_at = (row_y * CORES + row_core) * width
            row_first = frow_at * (CORES * y_size * width) + row_at
            for c in range(x_size):
                column_at = lax.rem(frow_at + c, x_size)
                column_first = (
                    column_at * (CORES * y_size) + y_at * CORES + core_at
                ) * width
                keep = row_first + row_iota <= column_first + column_iota
                block = total[r * width:(r + 1) * width, c * width:(c + 1) * width]
                out_ref[
                    pl.ds(pl.multiple_of(row_at, width), width),
                    pl.ds(pl.multiple_of(column_at * width, width), width),
                ] = jnp.where(keep, block * scale, 0.0)


def gram_tile(columns, rows, place, scale):
    depth, width = columns[0].shape
    steps = 4
    x_size, y_size = len(columns), len(rows) // CORES
    shape = (len(rows) * width, x_size * width)
    block = pl.BlockSpec((depth // steps, width), lambda i, place: (i, 0))
    return pl.pallas_call(
        functools.partial(gram_kernel, scale, steps, x_size, y_size),
        out_shape=jax.ShapeDtypeStruct(shape, jnp.float32),
        grid_spec=pltpu.PrefetchScalarGridSpec(
            num_scalar_prefetch=1,
            grid=(steps,),
            in_specs=[block] * (len(columns) + len(rows)),
            out_specs=pl.BlockSpec(shape, lambda i, place: (0, 0)),
            scratch_shapes=[pltpu.VMEM(shape, jnp.float32)],
        ),
        compiler_params=pltpu.CompilerParams(vmem_limit_bytes=32 * 1024 * 1024),
        cost_estimate=pl.CostEstimate(
            flops=2 * depth * shape[0] * shape[1],
            bytes_accessed=2 * depth * (shape[0] + shape[1]) + 4 * shape[0] * shape[1],
            transcendentals=0,
        ),
    )(place, *columns, *rows)


def score_kernel(groups, table, tests_ref, trains_ref, out_ref):
    share = TB // groups
    per_step = 8 // share
    for first in range(0, PAIRS, per_step):
        parts = []
        for slot in range(first, first + per_step):
            scores = lax.dot_general(
                tests_ref[table[0, slot]],
                trains_ref[table[1, slot]],
                (((1,), (1,)), ((), ())),
                preferred_element_type=jnp.float32,
            )
            parts.append(scores.reshape(groups, share, TB))
        out_ref[:, share * first:share * (first + per_step), :] = jnp.concatenate(parts, axis=1)


def pair_partials(tests, trains, table, groups):
    shape = (groups, PAIRS * TB // groups, TB)
    return pl.pallas_call(
        functools.partial(score_kernel, groups),
        out_shape=jax.ShapeDtypeStruct(shape, jnp.float32),
        grid_spec=pltpu.PrefetchScalarGridSpec(
            num_scalar_prefetch=1,
            grid=(1,),
            in_specs=[
                pl.BlockSpec(tests.shape, lambda i, table: (0, 0, 0)),
                pl.BlockSpec(trains.shape, lambda i, table: (0, 0, 0)),
            ],
            out_specs=pl.BlockSpec(shape, lambda i, table: (0, 0, 0)),
        ),
        compiler_params=pltpu.CompilerParams(vmem_limit_bytes=32 * 1024 * 1024),
    )(table, tests, trains)


def shift(axis, by):
    size = lax.axis_size(axis)
    return [((at + by) % size, at) for at in range(size)]


def shards(feature_slab, test_preconditioned, train_weight, pair_tests, pair_trains, pair_counts):
    slab_rows, feat_width = feature_slab.shape
    row_groups = lax.axis_size("frow")
    col_groups = lax.axis_size("fcol")
    corpus_size = lax.axis_size("corpus")
    frow_at = lax.axis_index("frow")
    fcol_at = lax.axis_index("fcol")

    blocks_held = test_preconditioned.shape[0] // TB
    test_ids = pair_tests[0]
    train_ids = pair_trains[0]
    slot_ids = jnp.arange(PAIRS, dtype=jnp.int32)
    is_live = slot_ids < pair_counts[0]
    holder = test_ids // blocks_held
    same = (holder[:, None] == holder[None, :]) & is_live[None, :]
    rank = jnp.sum(same & (slot_ids[None, :] < slot_ids[:, None]), axis=1).astype(jnp.int32)
    place_at = holder * CAP + rank
    asked = is_live[:, None] & (place_at[:, None] == jnp.arange(corpus_size * CAP)[None, :])
    wants = jnp.sum(jnp.where(asked, (test_ids % blocks_held)[:, None], 0), axis=0)
    wanted = lax.all_to_all(
        wants.astype(jnp.int32).reshape(corpus_size, CAP), "corpus", 0, 0, tiled=True
    )

    columns = [feature_slab]
    for by in range(1, row_groups):
        columns.append(lax.ppermute(feature_slab, "frow", shift("frow", by)))
    rows = []
    swap = [(at, at ^ 1) for at in range(col_groups)]
    for by in range(col_groups // CORES):
        own = feature_slab
        if by:
            own = lax.ppermute(feature_slab, "fcol", shift("fcol", CORES * by))
        rows += [own, lax.ppermute(own, "fcol", swap)]
    place = jnp.stack([frow_at, fcol_at // CORES, fcol_at % CORES]).astype(jnp.int32)
    norm_scale = (slab_rows * corpus_size) ** (-0.5)
    tile = gram_tile(columns, rows, place, norm_scale)
    summed_tile = lax.psum_scatter(tile, "corpus", scatter_dimension=0, tiled=True)
    gram_upper = summed_tile.reshape(summed_tile.shape[0], row_groups, feat_width)

    test_blocks = test_preconditioned.reshape(blocks_held, TB, feat_width)
    picked = jnp.take(test_blocks, wanted.reshape(-1), axis=0, mode="clip")
    picked = picked.reshape(corpus_size, CAP * TB, feat_width)
    received = lax.all_to_all(picked, "corpus", 0, 0, tiled=True)
    received = received.reshape(corpus_size * CAP, TB, feat_width)
    table = jnp.stack([jnp.where(is_live, place_at, 0), train_ids]).astype(jnp.int32)
    groups = row_groups * col_groups
    partials = pair_partials(
        received, feature_slab.reshape(-1, TB, feat_width), table, groups
    )
    gathered = lax.all_to_all(partials, ("frow", "fcol"), 0, 0, tiled=True)
    summed = jnp.sum(gathered, axis=0).reshape(PAIRS, TB // groups, TB)
    column_weights = jnp.take(train_weight.reshape(-1, TB), train_ids, axis=0)
    pair_scores = (
        summed * column_weights[:, None, :] * is_live.astype(jnp.float32)[:, None, None]
    )
    return (gram_upper, pair_scores[None])


def solution(mesh):
    return jax.shard_map(
        shards,
        mesh=mesh,
        in_specs=(
            P("corpus", ("frow", "fcol")),
            P("corpus", ("frow", "fcol")),
            P("corpus"),
            P("corpus", None),
            P("corpus", None),
            P("corpus"),
        ),
        out_specs=(P(("frow", "corpus"), None, "fcol"), P("corpus", None, ("frow", "fcol"), None)),
        check_vma=False,
    )
```

time: 371 us -> 169 us (0.46)
  the two profiles are of different devices: /device:TPU:2 before, /device:TPU:8 now
where the time goes in v1:
time: 169 us; the launch traced here: 168 us
  waiting for transfers between devices  68.7 us (41%)
  starting transfers between devices  39 us (23%)
  blocking collectives  27.4 us (16%)
  between operations  15 us (9%)
  Pallas kernels  9.66 us (6%)
  local copies, waits for them, and re-layouts  5.15 us (3%)
  other arithmetic  3.26 us (2%)
    all_to_all x1, blocking collectives, shards(): lax.all_to_all(wants.astype(jnp.int32).reshape(corpus_size, CAP), 'corpus...  27.4 us
    reduce_scatter x1, waiting for transfers between devices, shards(): lax.psum_scatter(tile, 'corpus', scatter_dimension=0, tiled=True)  26.5 us
    all_to_all x1, waiting for transfers between devices, shards(): received = lax.all_to_all(picked, 'corpus', 0, 0, tiled=True)  24.8 us
    all_to_all x1, waiting for transfers between devices, shards(): gathered = lax.all_to_all(partials, ('frow', 'fcol'), 0, 0, tiled=True)  14.9 us
    ppermute x3, starting transfers between devices, shards(): own = lax.ppermute(feature_slab, 'fcol', shift('fcol', CORES * by))  13.2 us
    ppermute x4, starting transfers between devices, shards(): rows += [own, lax.ppermute(own, 'fcol', swap)]  8.66 us
    ppermute x3, starting transfers between devices, shards(): columns.append(lax.ppermute(feature_slab, 'frow', shift('frow', by)))  7.81 us
    pallas_call x1, Pallas kernels, gram_tile(): pl.pallas_call(functools.partial(gram_kernel, scale, steps, x_size, y_siz...  7.63 us
  transfers between devices with their start and end apart: 13, of which 4 were waited for; matrix products, arithmetic and copies ran while one was open for 4% of the time, Pallas kernels for 6%

profile of v1, /device:TPU:8, one launch (start us, length us, event | category | flops | bytes accessed | tf_op | source)
XLA Modules:
  0.0 168.1 jit_solution(6390745614104528992)
XLA Ops:
  7.2 7.9 %collective-permute-start.4 = (bf16[2048,128]{1,0:T(8,128)(2,1)}, bf16[2048,128]{1,0:T(8,128)(2,1)S(1)}, u32[]{:S(2)}, u32[]{:S(2)}) collective-permute-start(bf16[2048,128]{1,0:T(8,128)(2,1)} %refs_4_.1), channel_id=1, source_target_pairs={{2,0},{3,1},{4,2},{5,3},{6,4},{7,5},{0,6},{1,7},{10,8},{11,9},{12,... | collective-permute-start | bytes 1572872 | tf_op jit(solution)/shard_map/ppermute | solution.py:153
  15.1 1.9 %collective-permute-start.6 = (bf16[2048,128]{1,0:T(8,128)(2,1)}, bf16[2048,128]{1,0:T(8,128)(2,1)S(1)}, u32[]{:S(2)}, u32[]{:S(2)}) collective-permute-start(bf16[2048,128]{1,0:T(8,128)(2,1)} %refs_4_.1), channel_id=1, source_target_pairs={{4,0},{5,1},{6,2},{7,3},{0,4},{1,5},{2,6},{3,7},{12,8},{13,9},{14,... | collective-permute-start | bytes 1572872 | tf_op jit(solution)/shard_map/ppermute | solution.py:153
  17.0 3.4 %collective-permute-start.8 = (bf16[2048,128]{1,0:T(8,128)(2,1)}, bf16[2048,128]{1,0:T(8,128)(2,1)S(1)}, u32[]{:S(2)}, u32[]{:S(2)}) collective-permute-start(bf16[2048,128]{1,0:T(8,128)(2,1)} %refs_4_.1), channel_id=1, source_target_pairs={{6,0},{7,1},{0,2},{1,3},{2,4},{3,5},{4,6},{5,7},{14,8},{15,9},{8,1... | collective-permute-start | bytes 1572872 | tf_op jit(solution)/shard_map/ppermute | solution.py:153
  20.4 2.3 %collective-permute-start = (bf16[2048,128]{1,0:T(8,128)(2,1)}, bf16[2048,128]{1,0:T(8,128)(2,1)}, u32[]{:S(2)}, u32[]{:S(2)}) collective-permute-start(bf16[2048,128]{1,0:T(8,128)(2,1)} %refs_4_.1), channel_id=1, source_target_pairs={{8,0},{16,8},{24,16},{0,24},{9,1},{17,9},{25,17},{1,25},{10,2},{18... | collective-permute-start | bytes 1572872 | tf_op jit(solution)/shard_map/ppermute | solution.py:147
  22.7 2.7 %collective-permute-start.1 = (bf16[2048,128]{1,0:T(8,128)(2,1)}, bf16[2048,128]{1,0:T(8,128)(2,1)}, u32[]{:S(2)}, u32[]{:S(2)}) collective-permute-start(bf16[2048,128]{1,0:T(8,128)(2,1)} %refs_4_.1), channel_id=1, source_target_pairs={{16,0},{24,8},{0,16},{8,24},{17,1},{25,9},{1,17},{9,25},{18,2},{26... | collective-permute-start | bytes 1572872 | tf_op jit(solution)/shard_map/ppermute | solution.py:147
  25.4 0.7 and_select_fusion
  27.8 27.4 %all_to_all.19 = s32[16,1,2]{2,1,0:T(1,128)S(1)} all-to-all(s32[16,1,2]{2,1,0:T(1,128)S(1)} %bitcast.47), channel_id=1, replica_groups=mesh['corpus'=16,'frow'=4,'fcol'=8] {'corpus'}, dimensions={0} | all-to-all | bytes 256 | tf_op jit(solution)/shard_map/all_to_all | solution.py:141
  55.7 0.7 reduce.3
  56.5 1.7 gather_fusion
  58.2 3.7 %all-to-all-start.1 = ((bf16[16,256,128]{2,1,0:T(8,128)(2,1)}), bf16[16,256,128]{2,1,0:T(8,128)(2,1)S(1)}, u32[]{:S(2)}, u32[]{:S(2)}) async-start(bf16[16,256,128]{2,1,0:T(8,128)(2,1)} %bitcast.44), calls=%async_computation.2 | async-start | bytes 2097152 | tf_op jit(solution)/shard_map/all_to_all | solution.py:164
  61.9 2.8 %collective-permute-start.2 = (bf16[2048,128]{1,0:T(8,128)(2,1)S(1)}, bf16[2048,128]{1,0:T(8,128)(2,1)}, u32[]{:S(2)}, u32[]{:S(2)}) collective-permute-start(bf16[2048,128]{1,0:T(8,128)(2,1)S(1)} %copy-done.1), channel_id=1, source_target_pairs={{24,0},{0,8},{8,16},{16,24},{25,1},{1,9},{9,17},{17,25},{26,2},{2,... | collective-permute-start | bytes 1572872 | tf_op jit(solution)/shard_map/ppermute | solution.py:147
  64.7 1.9 %collective-permute-start.3 = (bf16[2048,128]{1,0:T(8,128)(2,1)S(1)}, bf16[2048,128]{1,0:T(8,128)(2,1)}, u32[]{:S(2)}, u32[]{:S(2)}) collective-permute-start(bf16[2048,128]{1,0:T(8,128)(2,1)S(1)} %copy-done.1), channel_id=1, source_target_pairs={{0,1},{1,0},{2,3},{3,2},{4,5},{5,4},{6,7},{7,6},{8,9},{9,8},{10,11... | collective-permute-start | bytes 1572872 | tf_op jit(solution)/shard_map/ppermute | solution.py:154
  66.7 2.4 %collective-permute-start.5 = (bf16[2048,128]{1,0:T(8,128)(2,1)S(1)}, bf16[2048,128]{1,0:T(8,128)(2,1)}, u32[]{:S(2)}, u32[]{:S(2)}) collective-permute-start(bf16[2048,128]{1,0:T(8,128)(2,1)S(1)} %collective-permute-done.4.refs_6_), channel_id=1, source_target_pairs={{0,1},{1,0},{2,3},{3,2},{4,5},{5,4},{6,7},{7,6},{8,9},{9,8},{10,11... | collective-permute-start | bytes 1572872 | tf_op jit(solution)/shard_map/ppermute | solution.py:154
  69.1 1.9 %collective-permute-start.7 = (bf16[2048,128]{1,0:T(8,128)(2,1)S(1)}, bf16[2048,128]{1,0:T(8,128)(2,1)}, u32[]{:S(2)}, u32[]{:S(2)}) collective-permute-start(bf16[2048,128]{1,0:T(8,128)(2,1)S(1)} %collective-permute-done.6.refs_8_), channel_id=1, source_target_pairs={{0,1},{1,0},{2,3},{3,2},{4,5},{5,4},{6,7},{7,6},{8,9},{9,8},{10,11... | collective-permute-start | bytes 1572872 | tf_op jit(solution)/shard_map/ppermute | solution.py:154
  71.0 2.4 %collective-permute-start.9 = (bf16[2048,128]{1,0:T(8,128)(2,1)S(1)}, bf16[2048,128]{1,0:T(8,128)(2,1)}, u32[]{:S(2)}, u32[]{:S(2)}) collective-permute-start(bf16[2048,128]{1,0:T(8,128)(2,1)S(1)} %collective-permute-done.8.refs_10_), channel_id=1, source_target_pairs={{0,1},{1,0},{2,3},{3,2},{4,5},{5,4},{6,7},{7,6},{8,9},{9,8},{10,11... | collective-permute-start | bytes 1572872 | tf_op jit(solution)/shard_map/ppermute | solution.py:154
  73.5 2.4 %collective-permute-done.2.refs_3_ = bf16[2048,128]{1,0:T(8,128)(2,1)} collective-permute-done((bf16[2048,128]{1,0:T(8,128)(2,1)S(1)}, bf16[2048,128]{1,0:T(8,128)(2,1)}, u32[]{:S(2)}, u32[]{:S(2)}) %collective-permute-start.2) | collective-permute-done | bytes 524320 | tf_op jit(solution)/shard_map/ppermute | solution.py:147
  76.0 7.6 %shard_map.77 = f32[1024,512]{1,0:T(8,128)} custom-call(s32[3]{0:T(128)S(1)} %pad_add_fusion.1.place, bf16[2048,128]{1,0:T(8,128)(2,1)S(1)} %copy-done.1, bf16[2048,128]{1,0:T(8,128)(2,1)} %collective-permute-done.refs_1_, bf16[2048,128]{1,0:T(8,128)(2,1)} %collective-permute-done.1.refs_2_, bf16[2048,128]{1,0:T(8,128)(2,1)} %collective-permute-done.2.refs_3_, ...), custom_call_target="tpu_custom_call" | custom-call | flops 2147483648 | bytes 8388608 | tf_op jit(solution)/shard_map/pallas_call | solution.py:64
  84.3 24.8 %all-to-all-done.1 = bf16[16,256,128]{2,1,0:T(8,128)(2,1)S(1)} async-done(((bf16[16,256,128]{2,1,0:T(8,128)(2,1)}), bf16[16,256,128]{2,1,0:T(8,128)(2,1)S(1)}, u32[]{:S(2)}, u32[]{:S(2)}) %all-to-all-start.1) | async-done | bytes 1048608 | tf_op jit(solution)/shard_map/all_to_all | solution.py:164
  109.1 2.0 %shard_map.78 = f32[32,64,128]{2,1,0:T(8,128)} custom-call(s32[2,16]{1,0:T(2,128)S(1)} %pad_add_fusion.table, bf16[32,128,128]{2,1,0:T(8,128)(2,1)S(1)} %bitcast.43, bf16[16,128,128]{2,1,0:T(8,128)(2,1)S(1)} %bitcast.42), custom_call_target="tpu_custom_call" | custom-call | tf_op jit(solution)/shard_map/pallas_call | solution.py:101
  111.2 5.6 %all-to-all-start.2 = ((f32[32,64,128]{2,1,0:T(8,128)}), f32[32,64,128]{2,1,0:T(8,128)S(1)}, u32[]{:S(2)}, u32[]{:S(2)}) async-start(f32[32,64,128]{2,1,0:T(8,128)} %shard_map.78), calls=%async_computation.3 | async-start | bytes 2097152 | tf_op jit(solution)/shard_map/all_to_all | solution.py:171
  117.5 14.9 %all-to-all-done.2 = f32[32,64,128]{2,1,0:T(8,128)S(1)} async-done(((f32[32,64,128]{2,1,0:T(8,128)}), f32[32,64,128]{2,1,0:T(8,128)S(1)}, u32[]{:S(2)}, u32[]{:S(2)}) %all-to-all-start.2) | async-done | bytes 1048608 | tf_op jit(solution)/shard_map/all_to_all | solution.py:171
  132.4 0.7 multiply_multiply_fusion
  133.1 26.5 %reduce-scatter.2.cloned.1.call-done = f32[64,512]{1,0:T(8,128)} async-done(((f32[1024,512]{1,0:T(8,128)}), f32[64,512]{1,0:T(8,128)}) %reduce-scatter.2.cloned.1.call-update) | async-done | bytes 131088 | tf_op jit(solution)/shard_map/reduce_scatter | solution.py:158
  159.7 1.6 reshape.172
  (40 shorter events, 3.2 us)
Async XLA Ops:
  7.2 49.3 %copy-start = (bf16[1024,128]{1,0:T(8,128)(2,1)S(1)}, bf16[1024,128]{1,0:T(8,128)(2,1)}, u32[]{:S(2)}) copy-start(bf16[1024,128]{1,0:T(8,128)(2,1)} %param.7) | copy-start | bytes 786436
  7.2 54.7 %collective-permute-start.4 = (bf16[2048,128]{1,0:T(8,128)(2,1)}, bf16[2048,128]{1,0:T(8,128)(2,1)S(1)}, u32[]{:S(2)}, u32[]{:S(2)}) collective-permute-start(bf16[2048,128]{1,0:T(8,128)(2,1)} %refs_4_.1), channel_id=1, source_target_pairs={{2,0},{3,1},{4,2},{5,3},{6,4},{7,5},{0,6},{1,7},{10,8},{11,9},{12,... | collective-permute-start | bytes 1572872 | tf_op jit(solution)/shard_map/ppermute | solution.py:153
  15.1 49.7 %collective-permute-start.6 = (bf16[2048,128]{1,0:T(8,128)(2,1)}, bf16[2048,128]{1,0:T(8,128)(2,1)S(1)}, u32[]{:S(2)}, u32[]{:S(2)}) collective-permute-start(bf16[2048,128]{1,0:T(8,128)(2,1)} %refs_4_.1), channel_id=1, source_target_pairs={{4,0},{5,1},{6,2},{7,3},{0,4},{1,5},{2,6},{3,7},{12,8},{13,9},{14,... | collective-permute-start | bytes 1572872 | tf_op jit(solution)/shard_map/ppermute | solution.py:153
  17.0 49.7 %collective-permute-start.8 = (bf16[2048,128]{1,0:T(8,128)(2,1)}, bf16[2048,128]{1,0:T(8,128)(2,1)S(1)}, u32[]{:S(2)}, u32[]{:S(2)}) collective-permute-start(bf16[2048,128]{1,0:T(8,128)(2,1)} %refs_4_.1), channel_id=1, source_target_pairs={{6,0},{7,1},{0,2},{1,3},{2,4},{3,5},{4,6},{5,7},{14,8},{15,9},{8,1... | collective-permute-start | bytes 1572872 | tf_op jit(solution)/shard_map/ppermute | solution.py:153
  20.4 48.7 %collective-permute-start = (bf16[2048,128]{1,0:T(8,128)(2,1)}, bf16[2048,128]{1,0:T(8,128)(2,1)}, u32[]{:S(2)}, u32[]{:S(2)}) collective-permute-start(bf16[2048,128]{1,0:T(8,128)(2,1)} %refs_4_.1), channel_id=1, source_target_pairs={{8,0},{16,8},{24,16},{0,24},{9,1},{17,9},{25,17},{1,25},{10,2},{18... | collective-permute-start | bytes 1572872 | tf_op jit(solution)/shard_map/ppermute | solution.py:147
  22.7 48.4 %collective-permute-start.1 = (bf16[2048,128]{1,0:T(8,128)(2,1)}, bf16[2048,128]{1,0:T(8,128)(2,1)}, u32[]{:S(2)}, u32[]{:S(2)}) collective-permute-start(bf16[2048,128]{1,0:T(8,128)(2,1)} %refs_4_.1), channel_id=1, source_target_pairs={{16,0},{24,8},{0,16},{8,24},{17,1},{25,9},{1,17},{9,25},{18,2},{26... | collective-permute-start | bytes 1572872 | tf_op jit(solution)/shard_map/ppermute | solution.py:147
  56.5 5.4 %copy-start.1 = (bf16[2048,128]{1,0:T(8,128)(2,1)S(1)}, bf16[2048,128]{1,0:T(8,128)(2,1)}, u32[]{:S(2)}) copy-start(bf16[2048,128]{1,0:T(8,128)(2,1)} %refs_4_.1) | copy-start | bytes 1572868
  58.2 50.9 %all-to-all-start.1 = ((bf16[16,256,128]{2,1,0:T(8,128)(2,1)}), bf16[16,256,128]{2,1,0:T(8,128)(2,1)S(1)}, u32[]{:S(2)}, u32[]{:S(2)}) async-start(bf16[16,256,128]{2,1,0:T(8,128)(2,1)} %bitcast.44), calls=%async_computation.2 | async-start | bytes 2097152 | tf_op jit(solution)/shard_map/all_to_all | solution.py:164
  61.8 97.8 %reduce-scatter.2.cloned.1.call-start = ((), (), s32[]{:S(2)}) async-start(), calls=%async_computation.4 | async-start | bytes 2228224 | tf_op jit(solution)/shard_map/reduce_scatter | solution.py:158
  61.9 14.0 %collective-permute-start.2 = (bf16[2048,128]{1,0:T(8,128)(2,1)S(1)}, bf16[2048,128]{1,0:T(8,128)(2,1)}, u32[]{:S(2)}, u32[]{:S(2)}) collective-permute-start(bf16[2048,128]{1,0:T(8,128)(2,1)S(1)} %copy-done.1), channel_id=1, source_target_pairs={{24,0},{0,8},{8,16},{16,24},{25,1},{1,9},{9,17},{17,25},{26,2},{2,... | collective-permute-start | bytes 1572872 | tf_op jit(solution)/shard_map/ppermute | solution.py:147
  64.7 11.2 %collective-permute-start.3 = (bf16[2048,128]{1,0:T(8,128)(2,1)S(1)}, bf16[2048,128]{1,0:T(8,128)(2,1)}, u32[]{:S(2)}, u32[]{:S(2)}) collective-permute-start(bf16[2048,128]{1,0:T(8,128)(2,1)S(1)} %copy-done.1), channel_id=1, source_target_pairs={{0,1},{1,0},{2,3},{3,2},{4,5},{5,4},{6,7},{7,6},{8,9},{9,8},{10,11... | collective-permute-start | bytes 1572872 | tf_op jit(solution)/shard_map/ppermute | solution.py:154
  66.7 9.3 %collective-permute-start.5 = (bf16[2048,128]{1,0:T(8,128)(2,1)S(1)}, bf16[2048,128]{1,0:T(8,128)(2,1)}, u32[]{:S(2)}, u32[]{:S(2)}) collective-permute-start(bf16[2048,128]{1,0:T(8,128)(2,1)S(1)} %collective-permute-done.4.refs_6_), channel_id=1, source_target_pairs={{0,1},{1,0},{2,3},{3,2},{4,5},{5,4},{6,7},{7,6},{8,9},{9,8},{10,11... | collective-permute-start | bytes 1572872 | tf_op jit(solution)/shard_map/ppermute | solution.py:154
  69.1 6.9 %collective-permute-start.7 = (bf16[2048,128]{1,0:T(8,128)(2,1)S(1)}, bf16[2048,128]{1,0:T(8,128)(2,1)}, u32[]{:S(2)}, u32[]{:S(2)}) collective-permute-start(bf16[2048,128]{1,0:T(8,128)(2,1)S(1)} %collective-permute-done.6.refs_8_), channel_id=1, source_target_pairs={{0,1},{1,0},{2,3},{3,2},{4,5},{5,4},{6,7},{7,6},{8,9},{9,8},{10,11... | collective-permute-start | bytes 1572872 | tf_op jit(solution)/shard_map/ppermute | solution.py:154
  71.0 4.9 %collective-permute-start.9 = (bf16[2048,128]{1,0:T(8,128)(2,1)S(1)}, bf16[2048,128]{1,0:T(8,128)(2,1)}, u32[]{:S(2)}, u32[]{:S(2)}) collective-permute-start(bf16[2048,128]{1,0:T(8,128)(2,1)S(1)} %collective-permute-done.8.refs_10_), channel_id=1, source_target_pairs={{0,1},{1,0},{2,3},{3,2},{4,5},{5,4},{6,7},{7,6},{8,9},{9,8},{10,11... | collective-permute-start | bytes 1572872 | tf_op jit(solution)/shard_map/ppermute | solution.py:154
  83.6 0.7 copy-start.3
  83.6 0.7 copy-start.4
  109.1 7.7 %copy-start.2 = (f32[2048]{0:T(1024)S(1)}, f32[2048]{0:T(1024)}, u32[]{:S(2)}) copy-start(f32[2048]{0:T(1024)} %param.8) | copy-start | bytes 24580
  111.2 21.2 %all-to-all-start.2 = ((f32[32,64,128]{2,1,0:T(8,128)}), f32[32,64,128]{2,1,0:T(8,128)S(1)}, u32[]{:S(2)}, u32[]{:S(2)}) async-start(f32[32,64,128]{2,1,0:T(8,128)} %shard_map.78), calls=%async_computation.3 | async-start | bytes 2097152 | tf_op jit(solution)/shard_map/all_to_all | solution.py:171
Sparse Core Ops, SparseCore 0:
  83.8 75.8 reduce-scatter.1

commit v2 on v0

v2 whole, which is shorter than its diff:
```python
import functools

import jax
import jax.numpy as jnp
from jax import lax
from jax.experimental import pallas as pl
from jax.experimental.pallas import tpu as pltpu
from jax.sharding import PartitionSpec as P

TB = 128
PAIRS = 16
CAP = 2
CORES = 2
ID_ROWS = 16
VMEM_BYTES = 56 * 1024 * 1024


def gram_kernel(scale, x_size, place, rows_ref, *refs):
    out_ref = refs[-1]
    depth, width = rows_ref.shape[1], out_ref.shape[1]
    frow_at, fcol_at, col_groups = place[0], place[1], place[2]
    columns = jnp.concatenate([ref[...] for ref in refs[:-1]], axis=1)
    product = lax.dot_general(
        rows_ref[...], columns, (((0,), (0,)), ((), ())), preferred_element_type=jnp.float32
    )
    row_first = frow_at * col_groups * width + pl.program_id(0) * depth
    iota = [lax.broadcasted_iota(jnp.int32, (depth, width), axis) for axis in (0, 1)]
    for c in range(x_size):
        column_at = lax.rem(frow_at + c, x_size)
        column_first = (column_at * col_groups + fcol_at) * width
        keep = row_first + iota[0] <= column_first + iota[1]
        block = product[:, c * width:(c + 1) * width]
        out_ref[pl.ds(column_at, depth, stride=x_size), :] = jnp.where(keep, block * scale, 0.0)


def gram_tile(rows, columns, place, scale):
    depth, width = columns[0].shape
    x_size, panel = len(columns), rows.shape[1]
    step = 2 * width
    shape = (panel * x_size, width)
    return pl.pallas_call(
        functools.partial(gram_kernel, scale, x_size),
        out_shape=jax.ShapeDtypeStruct(shape, jnp.float32),
        grid_spec=pltpu.PrefetchScalarGridSpec(
            num_scalar_prefetch=1,
            grid=(panel // step,),
            in_specs=[pl.BlockSpec((depth, step), lambda i, place: (0, i))]
            + [pl.BlockSpec((depth, width), lambda i, place: (0, 0))] * x_size,
            out_specs=pl.BlockSpec((step * x_size, width), lambda i, place: (i, 0)),
        ),
        compiler_params=pltpu.CompilerParams(vmem_limit_bytes=VMEM_BYTES),
        cost_estimate=pl.CostEstimate(
            flops=32 * depth * shape[0] * width,
            bytes_accessed=2 * depth * (panel + x_size * width) + 4 * shape[0] * width,
            transcendentals=0,
        ),
    )(place, rows, *columns)


def offer_kernel(held, tests, trains, count, trains_ref, out_ref, places, seen, block_of, id_of):
    holders = out_ref.shape[0]
    lane = lax.broadcasted_iota(jnp.int32, (ID_ROWS, TB), 1)

    @pl.loop(0, holders)
    def _(h):
        seen[h] = 0
        for r in range(CAP):
            block_of[h, r] = 0
            id_of[h, r] = 0

    @pl.loop(0, PAIRS)
    def _(slot):
        places[0, slot] = 0

        @pl.when(slot < count[0])
        def _():
            holder = tests[0, slot] // held
            rank = seen[holder]
            block_of[holder, rank] = trains[0, slot]
            id_of[holder, rank] = tests[0, slot] - holder * held
            places[0, slot] = holder * CAP + rank
            seen[holder] = rank + 1

    for h in range(holders):
        ids = jnp.zeros((ID_ROWS, TB), jnp.int32)
        for r in range(CAP):
            out_ref[h, r * TB:(r + 1) * TB, :] = trains_ref[block_of[h, r]]
            ids = jnp.where(lane == r, id_of[h, r], ids)
        out_ref[h, CAP * TB:, :] = ids.astype(jnp.float32).astype(out_ref.dtype)


def offers(trains, pair_tests, pair_trains, pair_counts, holders, held):
    smem = pl.BlockSpec(memory_space=pltpu.SMEM)
    shape = (holders, CAP * TB + ID_ROWS, trains.shape[-1])
    return pl.pallas_call(
        functools.partial(offer_kernel, held),
        out_shape=(
            jax.ShapeDtypeStruct(shape, trains.dtype),
            jax.ShapeDtypeStruct((1, PAIRS), jnp.int32),
        ),
        in_specs=[smem] * 3 + [pl.BlockSpec(memory_space=pltpu.VMEM)],
        out_specs=(pl.BlockSpec(memory_space=pltpu.VMEM), smem),
        scratch_shapes=[pltpu.SMEM((holders,), jnp.int32)]
        + [pltpu.SMEM((holders, CAP), jnp.int32)] * 2,
    )(pair_tests, pair_trains, pair_counts, trains)


def score_kernel(groups, ids, core, offered_ref, tests_ref, send_ref, keep_ref):
    share = TB // groups
    for asker in range(offered_ref.shape[0]):
        sent, kept = [], []
        for r in range(CAP):
            scores = lax.dot_general(
                tests_ref[ids[asker, r]],
                offered_ref[asker, r * TB:(r + 1) * TB, :],
                (((1,), (1,)), ((), ())),
                preferred_element_type=jnp.float32,
            )
            scores = scores.reshape(groups // CORES, CORES, share, TB)
            first, second = scores[:, 0], scores[:, 1]
            kept.append(jnp.where(core[0] == 0, first, second))
            sent.append(jnp.where(core[0] == 0, second, first))
        rows = slice(asker * CAP * share, (asker + 1) * CAP * share)
        send_ref[:, rows, :] = jnp.concatenate(sent, axis=1)
        keep_ref[:, rows, :] = jnp.concatenate(kept, axis=1)


def pair_partials(offered, tests, ids, core, groups):
    askers = offered.shape[0]
    shape = (groups // CORES, askers * CAP * TB // groups, TB)
    out_block = pl.BlockSpec(shape, lambda i, ids, core: (0, 0, 0))
    return pl.pallas_call(
        functools.partial(score_kernel, groups),
        out_shape=[jax.ShapeDtypeStruct(shape, jnp.float32)] * 2,
        grid_spec=pltpu.PrefetchScalarGridSpec(
            num_scalar_prefetch=2,
            grid=(1,),
            in_specs=[
                pl.BlockSpec(offered.shape, lambda i, ids, core: (0, 0, 0)),
                pl.BlockSpec(tests.shape, lambda i, ids, core: (0, 0, 0)),
            ],
            out_specs=[out_block] * 2,
        ),
        compiler_params=pltpu.CompilerParams(vmem_limit_bytes=VMEM_BYTES),
    )(ids, core, offered, tests)


def weigh_kernel(places, trains, count, scores_ref, weights_ref, out_ref):
    for slot in range(PAIRS):
        scores = scores_ref[places[0, slot]]
        weights = weights_ref[pl.ds(trains[0, slot], 1), :]
        out_ref[slot] = jnp.where(slot < count[0], scores * weights, 0.0)


def weigh(scores, weights, places, pair_trains, pair_counts):
    smem = pl.BlockSpec(memory_space=pltpu.SMEM)
    vmem = pl.BlockSpec(memory_space=pltpu.VMEM)
    return pl.pallas_call(
        weigh_kernel,
        out_shape=jax.ShapeDtypeStruct((PAIRS,) + scores.shape[1:], jnp.float32),
        in_specs=[smem] * 3 + [vmem] * 2,
        out_specs=vmem,
    )(places, pair_trains, pair_counts, scores, weights)


def shift(axis, by):
    size = lax.axis_size(axis)
    return [((at + by) % size, at) for at in range(size)]


def shards(feature_slab, test_preconditioned, train_weight, pair_tests, pair_trains, pair_counts):
    slab_rows, feat_width = feature_slab.shape
    row_groups = lax.axis_size("frow")
    col_groups = lax.axis_size("fcol")
    corpus_size = lax.axis_size("corpus")
    frow_at = lax.axis_index("frow")
    fcol_at = lax.axis_index("fcol")

    held = test_preconditioned.shape[0] // TB
    offered, places = offers(
        feature_slab.reshape(-1, TB, feat_width), pair_tests, pair_trains, pair_counts, corpus_size, held
    )
    offered = lax.all_to_all(offered, "corpus", 0, 0, tiled=True)
    ids = offered[:, CAP * TB, :CAP].astype(jnp.int32)

    panel = lax.all_gather(feature_slab, "fcol", axis=1, tiled=True)
    columns = [feature_slab] + [
        lax.ppermute(feature_slab, "frow", shift("frow", by)) for by in range(1, row_groups)
    ]
    place = jnp.stack([frow_at, fcol_at, jnp.int32(col_groups)]).astype(jnp.int32)
    norm_scale = (slab_rows * corpus_size) ** (-0.5)
    tile = gram_tile(panel, columns, place, norm_scale)
    summed_tile = lax.psum_scatter(tile, "corpus", scatter_dimension=0, tiled=True)
    gram_upper = summed_tile.reshape(-1, row_groups, feat_width)

    groups = row_groups * col_groups
    core = (fcol_at % CORES).astype(jnp.int32).reshape(1)
    send, keep = pair_partials(
        offered, test_preconditioned.reshape(held, TB, feat_width), ids, core, groups
    )
    partials = keep + lax.ppermute(send, "fcol", [(at, at ^ 1) for at in range(col_groups)])
    same_core = [list(range(at, groups, CORES)) for at in range(CORES)]
    gathered = lax.all_to_all(
        partials, ("frow", "fcol"), 0, 0, axis_index_groups=same_core, tiled=True
    )
    summed = jnp.sum(gathered, axis=0)
    returned = lax.all_to_all(summed.reshape(corpus_size, -1, TB), "corpus", 0, 0, tiled=True)
    pair_scores = weigh(
        returned.reshape(corpus_size * CAP, TB // groups, TB),
        train_weight.reshape(-1, TB), places, pair_trains, pair_counts,
    )
    return (gram_upper, pair_scores[None])


def solution(mesh):
    return jax.shard_map(
        shards,
        mesh=mesh,
        in_specs=(
            P("corpus", ("frow", "fcol")),
            P("corpus", ("frow", "fcol")),
            P("corpus"),
            P("corpus", None),
            P("corpus", None),
            P("corpus"),
        ),
        out_specs=(P(("frow", "corpus"), None, "fcol"), P("corpus", None, ("frow", "fcol"), None)),
        check_vma=False,
    )
```

time: 371 us -> 153 us (0.41)
  the two profiles are of different devices: /device:TPU:2 before, /device:TPU:8 now
where the time goes in v2:
time: 153 us; the launch traced here: 152 us
  waiting for transfers between devices  47.1 us (31%)
  blocking collectives  44.3 us (29%)
  starting transfers between devices  27.4 us (18%)
  Pallas kernels  15.7 us (10%)
  between operations  14.8 us (10%)
  other arithmetic  2.71 us (2%)
    all_to_all x1, waiting for transfers between devices, shards(): offered = lax.all_to_all(offered, 'corpus', 0, 0, tiled=True)  23 us
    all_to_all x1, blocking collectives, shards(): lax.all_to_all(partials, ('frow', 'fcol'), 0, 0, axis_index_groups=same_c...  22.6 us
    all_to_all x1, blocking collectives, shards(): lax.all_to_all(summed.reshape(corpus_size, -1, TB), 'corpus', 0, 0, tiled...  21.8 us
    all_gather x1, waiting for transfers between devices, shards(): panel = lax.all_gather(feature_slab, 'fcol', axis=1, tiled=True)  17.1 us
    all_to_all x1, starting transfers between devices, shards(): offered = lax.all_to_all(offered, 'corpus', 0, 0, tiled=True)  15.2 us
    ppermute x3, starting transfers between devices, shards(): lax.ppermute(feature_slab, 'frow', shift('frow', by))  10.2 us
    pallas_call x1, Pallas kernels, gram_tile(): pl.pallas_call(functools.partial(gram_kernel, scale, x_size), out_shape=j...  7.29 us
    pallas_call x1, Pallas kernels, pair_partials(): pl.pallas_call(functools.partial(score_kernel, groups), out_shape=[jax.Sh...  4.23 us
  transfers between devices with their start and end apart: 7, of which 4 were waited for; matrix products, arithmetic and copies ran while one was open for 2% of the time, Pallas kernels for 10%

profile of v2, /device:TPU:8, one launch (start us, length us, event | category | flops | bytes accessed | tf_op | source)
XLA Modules:
  0.0 152.4 jit_solution(7653846046214634453)
XLA Ops:
  7.2 0.0 all-gather.2.cloned.1.call-start
  7.2 0.7 all-gather.2.cloned.1.call-update
  7.9 4.7 %collective-permute-start = (bf16[2048,128]{1,0:T(8,128)(2,1)}, bf16[2048,128]{1,0:T(8,128)(2,1)S(1)}, u32[]{:S(2)}, u32[]{:S(2)}) collective-permute-start(bf16[2048,128]{1,0:T(8,128)(2,1)} %refs_0_.1), channel_id=1, source_target_pairs={{8,0},{16,8},{24,16},{0,24},{9,1},{17,9},{25,17},{1,25},{10,2},{18... | collective-permute-start | bytes 1572872 | tf_op jit(solution)/shard_map/ppermute | solution.py:188
  12.6 2.7 %collective-permute-start.1 = (bf16[2048,128]{1,0:T(8,128)(2,1)}, bf16[2048,128]{1,0:T(8,128)(2,1)S(1)}, u32[]{:S(2)}, u32[]{:S(2)}) collective-permute-start(bf16[2048,128]{1,0:T(8,128)(2,1)} %refs_0_.1), channel_id=1, source_target_pairs={{16,0},{24,8},{0,16},{8,24},{17,1},{25,9},{1,17},{9,25},{18,2},{26... | collective-permute-start | bytes 1572872 | tf_op jit(solution)/shard_map/ppermute | solution.py:188
  15.3 2.8 %collective-permute-start.2 = (bf16[2048,128]{1,0:T(8,128)(2,1)}, bf16[2048,128]{1,0:T(8,128)(2,1)S(1)}, u32[]{:S(2)}, u32[]{:S(2)}) collective-permute-start(bf16[2048,128]{1,0:T(8,128)(2,1)} %refs_0_.1), channel_id=1, source_target_pairs={{24,0},{0,8},{8,16},{16,24},{25,1},{1,9},{9,17},{17,25},{26,2},{2,... | collective-permute-start | bytes 1572872 | tf_op jit(solution)/shard_map/ppermute | solution.py:188
  18.7 2.7 %shard_map.78 = (bf16[16,272,128]{2,1,0:T(8,128)(2,1)}, s32[1,16]{1,0:T(1,128)}) custom-call(s32[1,16]{1,0:T(1,128)} %tests.1, s32[1,16]{1,0:T(1,128)} %trains.3, s32[1]{0:T(128)S(6)} %copy.13.count, bf16[16,128,128]{2,1,0:T(8,128)(2,1)} %bitcast.11), custom_call_target="tpu_custom_call" | custom-call | tf_op jit(solution)/shard_map/pallas_call | solution.py:95
  21.4 15.2 %all-to-all-start = ((bf16[16,272,128]{2,1,0:T(8,128)(2,1)}), bf16[16,272,128]{2,1,0:T(8,128)(2,1)S(1)}, u32[]{:S(2)}, u32[]{:S(2)}) async-start(bf16[16,272,128]{2,1,0:T(8,128)(2,1)} %get-tuple-element.7), calls=%async_computation.1 | async-start | bytes 2228224 | tf_op jit(solution)/shard_map/all_to_all | solution.py:183
  36.7 0.0 reduce-scatter.2.cloned.1.call-start
  36.7 0.7 pad_add_fusion.place
  37.4 3.4 %collective-permute-done.2.refs_3_ = bf16[2048,128]{1,0:T(8,128)(2,1)S(1)} collective-permute-done((bf16[2048,128]{1,0:T(8,128)(2,1)}, bf16[2048,128]{1,0:T(8,128)(2,1)S(1)}, u32[]{:S(2)}, u32[]{:S(2)}) %collective-permute-start.2) | collective-permute-done | bytes 524320 | tf_op jit(solution)/shard_map/ppermute | solution.py:188
  40.8 17.1 %all-gather.2.cloned.1.call-done.rows_ref = bf16[2048,1024]{1,0:T(8,128)(2,1)} async-done(((bf16[2048,128]{1,0:T(8,128)(2,1)}), bf16[2048,1024]{1,0:T(8,128)(2,1)}) %all-gather.2.cloned.1.call-update) | async-done | bytes 4194320 | tf_op jit(solution)/shard_map/all_gather | solution.py:186
  58.0 7.3 %shard_map.77 = f32[4096,128]{1,0:T(8,128)} custom-call(s32[3]{0:T(128)} %pad_add_fusion.place, bf16[2048,1024]{1,0:T(8,128)(2,1)} %all-gather.2.cloned.1.call-done.rows_ref, bf16[2048,128]{1,0:T(8,128)(2,1)} %refs_0_.1, bf16[2048,128]{1,0:T(8,128)(2,1)} %copy-done.1, bf16[2048,128]{1,0:T(8,128)(2,1)} %copy-done.2, bf16[2048,128]{1,0:T(8,128)(2,1)} %copy-done.3), custom_call_target="tpu_custom_call" | custom-call | flops 34359738368 | bytes 8388608 | tf_op jit(solution)/shard_map/pallas_call | solution.py:41
  65.2 0.0 reduce-scatter.2.cloned.1.call-update
  65.3 23.0 %all-to-all-done.offered_ref = bf16[16,272,128]{2,1,0:T(8,128)(2,1)S(1)} async-done(((bf16[16,272,128]{2,1,0:T(8,128)(2,1)}), bf16[16,272,128]{2,1,0:T(8,128)(2,1)S(1)}, u32[]{:S(2)}, u32[]{:S(2)}) %all-to-all-start) | async-done | bytes 1114144 | tf_op jit(solution)/shard_map/all_to_all | solution.py:183
  88.3 0.7 slice_convert_fusion
  89.0 0.4 copy-done
  89.3 4.2 %shard_map.79 = (f32[16,128,128]{2,1,0:T(8,128)}, f32[16,128,128]{2,1,0:T(8,128)}) custom-call(s32[16,2]{1,0:T(8,128)} %bitcast.15, s32[1]{0:T(128)} %bitcast.5.core, bf16[16,272,128]{2,1,0:T(8,128)(2,1)} %copy-done, bf16[8,128,128]{2,1,0:T(8,128)(2,1)} %bitcast.12), custom_call_target="tpu_custom_call" | custom-call | tf_op jit(solution)/shard_map/pallas_call | solution.py:132
  93.5 1.9 %collective-permute-start.3 = (f32[16,128,128]{2,1,0:T(8,128)}, f32[16,128,128]{2,1,0:T(8,128)S(1)}, u32[]{:S(2)}, u32[]{:S(2)}) collective-permute-start(f32[16,128,128]{2,1,0:T(8,128)} %get-tuple-element.9), channel_id=1, source_target_pairs={{0,1},{1,0},{2,3},{3,2},{4,5},{5,4},{6,7},{7,6},{8,9},{9,8},{10,11... | collective-permute-start | bytes 3145736 | tf_op jit(solution)/shard_map/ppermute | solution.py:201
  95.5 2.8 %collective-permute-done.3 = f32[16,128,128]{2,1,0:T(8,128)S(1)} collective-permute-done((f32[16,128,128]{2,1,0:T(8,128)}, f32[16,128,128]{2,1,0:T(8,128)S(1)}, u32[]{:S(2)}, u32[]{:S(2)}) %collective-permute-start.3) | collective-permute-done | bytes 1048608 | tf_op jit(solution)/shard_map/ppermute | solution.py:201
  98.3 1.3 add.10
  99.6 22.6 %all_to_all.15 = f32[16,128,128]{2,1,0:T(8,128)S(1)} all-to-all(f32[16,128,128]{2,1,0:T(8,128)S(1)} %add.10), channel_id=1, replica_groups={{0,2,4,6,8,10,12,14,16,18,20,22,24,26,28,30},{1,3,5,7,9,11,13,15,17,19,..., dimensions={0} | all-to-all | bytes 2097152 | tf_op jit(solution)/shard_map/all_to_all | solution.py:203
  122.2 0.1 reduce_sum.9
  122.3 21.8 %all_to_all.16 = f32[16,8,128]{2,1,0:T(8,128)} all-to-all(f32[16,8,128]{2,1,0:T(8,128)S(1)} %bitcast.13), channel_id=1, replica_groups=mesh['corpus'=16,'frow'=4,'fcol'=8] {'corpus'}, dimensions={0} | all-to-all | bytes 131072 | tf_op jit(solution)/shard_map/all_to_all | solution.py:207
  144.0 1.5 shard_map.80
  (10 shorter events, 0.0 us)
Async XLA Ops:
  7.2 50.8 %all-gather.2.cloned.1.call-start = ((), (), s32[]{:S(2)}) async-start(), calls=%async_computation.4 | async-start | bytes 4718592 | tf_op jit(solution)/shard_map/all_gather | solution.py:186
  7.9 29.5 %collective-permute-start = (bf16[2048,128]{1,0:T(8,128)(2,1)}, bf16[2048,128]{1,0:T(8,128)(2,1)S(1)}, u32[]{:S(2)}, u32[]{:S(2)}) collective-permute-start(bf16[2048,128]{1,0:T(8,128)(2,1)} %refs_0_.1), channel_id=1, source_target_pairs={{8,0},{16,8},{24,16},{0,24},{9,1},{17,9},{25,17},{1,25},{10,2},{18... | collective-permute-start | bytes 1572872 | tf_op jit(solution)/shard_map/ppermute | solution.py:188
  12.6 24.8 %collective-permute-start.1 = (bf16[2048,128]{1,0:T(8,128)(2,1)}, bf16[2048,128]{1,0:T(8,128)(2,1)S(1)}, u32[]{:S(2)}, u32[]{:S(2)}) collective-permute-start(bf16[2048,128]{1,0:T(8,128)(2,1)} %refs_0_.1), channel_id=1, source_target_pairs={{16,0},{24,8},{0,16},{8,24},{17,1},{25,9},{1,17},{9,25},{18,2},{26... | collective-permute-start | bytes 1572872 | tf_op jit(solution)/shard_map/ppermute | solution.py:188
  15.3 25.5 %collective-permute-start.2 = (bf16[2048,128]{1,0:T(8,128)(2,1)}, bf16[2048,128]{1,0:T(8,128)(2,1)S(1)}, u32[]{:S(2)}, u32[]{:S(2)}) collective-permute-start(bf16[2048,128]{1,0:T(8,128)(2,1)} %refs_0_.1), channel_id=1, source_target_pairs={{24,0},{0,8},{8,16},{16,24},{25,1},{1,9},{9,17},{17,25},{26,2},{2,... | collective-permute-start | bytes 1572872 | tf_op jit(solution)/shard_map/ppermute | solution.py:188
  21.4 66.9 %all-to-all-start = ((bf16[16,272,128]{2,1,0:T(8,128)(2,1)}), bf16[16,272,128]{2,1,0:T(8,128)(2,1)S(1)}, u32[]{:S(2)}, u32[]{:S(2)}) async-start(bf16[16,272,128]{2,1,0:T(8,128)(2,1)} %get-tuple-element.7), calls=%async_computation.1 | async-start | bytes 2228224 | tf_op jit(solution)/shard_map/all_to_all | solution.py:183
  36.7 108.9 %reduce-scatter.2.cloned.1.call-start = ((), (), s32[]{:S(2)}) async-start(), calls=%async_computation.5 | async-start | bytes 2228224 | tf_op jit(solution)/shard_map/reduce_scatter | solution.py:193
  37.4 20.6 %copy-start.1 = (bf16[2048,128]{1,0:T(8,128)(2,1)}, bf16[2048,128]{1,0:T(8,128)(2,1)S(1)}, u32[]{:S(2)}) copy-start(bf16[2048,128]{1,0:T(8,128)(2,1)S(1)} %collective-permute-done.refs_1_) | copy-start | bytes 1572868
  37.4 20.6 %copy-start.2 = (bf16[2048,128]{1,0:T(8,128)(2,1)}, bf16[2048,128]{1,0:T(8,128)(2,1)S(1)}, u32[]{:S(2)}) copy-start(bf16[2048,128]{1,0:T(8,128)(2,1)S(1)} %collective-permute-done.1.refs_2_) | copy-start | bytes 1572868
  40.8 17.2 %copy-start.3 = (bf16[2048,128]{1,0:T(8,128)(2,1)}, bf16[2048,128]{1,0:T(8,128)(2,1)S(1)}, u32[]{:S(2)}) copy-start(bf16[2048,128]{1,0:T(8,128)(2,1)S(1)} %collective-permute-done.2.refs_3_) | copy-start | bytes 1572868
  88.3 1.0 copy-start
  93.5 4.8 %collective-permute-start.3 = (f32[16,128,128]{2,1,0:T(8,128)}, f32[16,128,128]{2,1,0:T(8,128)S(1)}, u32[]{:S(2)}, u32[]{:S(2)}) collective-permute-start(f32[16,128,128]{2,1,0:T(8,128)} %get-tuple-element.9), channel_id=1, source_target_pairs={{0,1},{1,0},{2,3},{3,2},{4,5},{5,4},{6,7},{7,6},{8,9},{9,8},{10,11... | collective-permute-start | bytes 3145736 | tf_op jit(solution)/shard_map/ppermute | solution.py:201
Sparse Core Ops, SparseCore 0:
  10.1 47.7 all-gather.1
  65.4 75.4 reduce-scatter.1

commit v3 on v2

--- a/solution.py
+++ b/solution.py
@@ -36,7 +36,7 @@
 def gram_tile(rows, columns, place, scale):
     depth, width = columns[0].shape
     x_size, panel = len(columns), rows.shape[1]
-    step = 2 * width
+    step = 4 * width
     shape = (panel * x_size, width)
     return pl.pallas_call(
         functools.partial(gram_kernel, scale, x_size),
@@ -50,7 +50,7 @@
         ),
         compiler_params=pltpu.CompilerParams(vmem_limit_bytes=VMEM_BYTES),
         cost_estimate=pl.CostEstimate(
-            flops=32 * depth * shape[0] * width,
+            flops=2 * depth * shape[0] * width,
             bytes_accessed=2 * depth * (panel + x_size * width) + 4 * shape[0] * width,
             transcendentals=0,
         ),

time: 153 us -> 149 us (0.974)
  the two profiles are of different devices: /device:TPU:8 before, /device:TPU:30 now
where the time goes in v3:
time: 149 us; the launch traced here: 148 us
  waiting for transfers between devices  46.5 us (31%)
  blocking collectives  41.1 us (28%)
  starting transfers between devices  27.1 us (18%)
  Pallas kernels  15.1 us (10%)
  between operations  14.8 us (10%)
  other arithmetic  2.65 us (2%)
    all_to_all x1, blocking collectives, shards(): lax.all_to_all(summed.reshape(corpus_size, -1, TB), 'corpus', 0, 0, tiled...  20.9 us
    all_to_all x1, blocking collectives, shards(): lax.all_to_all(partials, ('frow', 'fcol'), 0, 0, axis_index_groups=same_c...  20.2 us
    ppermute x3, waiting for transfers between devices, shards(): lax.ppermute(feature_slab, 'frow', shift('frow', by))  19.9 us
    all_to_all x1, starting transfers between devices, shards(): offered = lax.all_to_all(offered, 'corpus', 0, 0, tiled=True)  15.3 us
    all_to_all x1, waiting for transfers between devices, shards(): offered = lax.all_to_all(offered, 'corpus', 0, 0, tiled=True)  14.7 us
    ppermute x3, starting transfers between devices, shards(): lax.ppermute(feature_slab, 'frow', shift('frow', by))  9.76 us
    reduce_scatter x1, waiting for transfers between devices, shards(): lax.psum_scatter(tile, 'corpus', scatter_dimension=0, tiled=True)  7.96 us
    pallas_call x1, Pallas kernels, gram_tile(): pl.pallas_call(functools.partial(gram_kernel, scale, x_size), out_shape=j...  6.66 us
  transfers between devices with their start and end apart: 7, of which 6 were waited for; matrix products, arithmetic and copies ran while one was open for 2% of the time, Pallas kernels for 10%

profile of v3, /device:TPU:30, one launch (start us, length us, event | category | flops | bytes accessed | tf_op | source)
XLA Modules:
  0.0 148.0 jit_solution(3117974190010543694)
XLA Ops:
  7.2 0.7 all-gather.2.cloned.1.call-update
  8.5 2.7 %shard_map.78 = (bf16[16,272,128]{2,1,0:T(8,128)(2,1)}, s32[1,16]{1,0:T(1,128)}) custom-call(s32[1,16]{1,0:T(1,128)} %tests.1, s32[1,16]{1,0:T(1,128)} %trains.3, s32[1]{0:T(128)S(6)} %copy.13.count, bf16[16,128,128]{2,1,0:T(8,128)(2,1)} %bitcast.11), custom_call_target="tpu_custom_call" | custom-call | tf_op jit(solution)/shard_map/pallas_call | solution.py:95
  11.3 15.3 %all-to-all-start = ((bf16[16,272,128]{2,1,0:T(8,128)(2,1)}), bf16[16,272,128]{2,1,0:T(8,128)(2,1)S(1)}, u32[]{:S(2)}, u32[]{:S(2)}) async-start(bf16[16,272,128]{2,1,0:T(8,128)(2,1)} %get-tuple-element.7), calls=%async_computation.1 | async-start | bytes 2228224 | tf_op jit(solution)/shard_map/all_to_all | solution.py:183
  26.7 2.7 %collective-permute-start = (bf16[2048,128]{1,0:T(8,128)(2,1)S(1)}, bf16[2048,128]{1,0:T(8,128)(2,1)S(1)}, u32[]{:S(2)}, u32[]{:S(2)}) collective-permute-start(bf16[2048,128]{1,0:T(8,128)(2,1)S(1)} %copy-done), channel_id=1, source_target_pairs={{8,0},{16,8},{24,16},{0,24},{9,1},{17,9},{25,17},{1,25},{10,2},{18... | collective-permute-start | bytes 1572872 | tf_op jit(solution)/shard_map/ppermute | solution.py:188
  29.4 3.0 %collective-permute-start.1 = (bf16[2048,128]{1,0:T(8,128)(2,1)S(1)}, bf16[2048,128]{1,0:T(8,128)(2,1)S(1)}, u32[]{:S(2)}, u32[]{:S(2)}) collective-permute-start(bf16[2048,128]{1,0:T(8,128)(2,1)S(1)} %copy-done), channel_id=1, source_target_pairs={{16,0},{24,8},{0,16},{8,24},{17,1},{25,9},{1,17},{9,25},{18,2},{26... | collective-permute-start | bytes 1572872 | tf_op jit(solution)/shard_map/ppermute | solution.py:188
  32.4 4.0 %collective-permute-start.2 = (bf16[2048,128]{1,0:T(8,128)(2,1)S(1)}, bf16[2048,128]{1,0:T(8,128)(2,1)S(1)}, u32[]{:S(2)}, u32[]{:S(2)}) collective-permute-start(bf16[2048,128]{1,0:T(8,128)(2,1)S(1)} %copy-done), channel_id=1, source_target_pairs={{24,0},{0,8},{8,16},{16,24},{25,1},{1,9},{9,17},{17,25},{26,2},{2,... | collective-permute-start | bytes 1572872 | tf_op jit(solution)/shard_map/ppermute | solution.py:188
  36.5 0.6 pad_add_fusion.place
  37.0 17.3 %collective-permute-done.refs_1_ = bf16[2048,128]{1,0:T(8,128)(2,1)S(1)} collective-permute-done((bf16[2048,128]{1,0:T(8,128)(2,1)S(1)}, bf16[2048,128]{1,0:T(8,128)(2,1)S(1)}, u32[]{:S(2)}, u32[]{:S(2)}) %collective-permute-start) | collective-permute-done | bytes 524320 | tf_op jit(solution)/shard_map/ppermute | solution.py:188
  54.4 2.5 %collective-permute-done.2.refs_3_ = bf16[2048,128]{1,0:T(8,128)(2,1)S(1)} collective-permute-done((bf16[2048,128]{1,0:T(8,128)(2,1)S(1)}, bf16[2048,128]{1,0:T(8,128)(2,1)S(1)}, u32[]{:S(2)}, u32[]{:S(2)}) %collective-permute-start.2) | collective-permute-done | bytes 524320 | tf_op jit(solution)/shard_map/ppermute | solution.py:188
  56.9 0.4 all-gather.2.cloned.1.call-done.rows_ref
  57.3 0.4 copy-done.4
  57.8 6.7 %shard_map.77 = f32[4096,128]{1,0:T(8,128)} custom-call(s32[3]{0:T(128)} %pad_add_fusion.place, bf16[2048,1024]{1,0:T(8,128)(2,1)} %all-gather.2.cloned.1.call-done.rows_ref, bf16[2048,128]{1,0:T(8,128)(2,1)} %refs_0_.1, bf16[2048,128]{1,0:T(8,128)(2,1)} %copy-done.2, bf16[2048,128]{1,0:T(8,128)(2,1)} %copy-done.3, bf16[2048,128]{1,0:T(8,128)(2,1)} %copy-done.4), custom_call_target="tpu_custom_call" | custom-call | flops 2147483648 | bytes 8388608 | tf_op jit(solution)/shard_map/pallas_call | solution.py:41
  64.5 14.7 %all-to-all-done.offered_ref = bf16[16,272,128]{2,1,0:T(8,128)(2,1)S(1)} async-done(((bf16[16,272,128]{2,1,0:T(8,128)(2,1)}), bf16[16,272,128]{2,1,0:T(8,128)(2,1)S(1)}, u32[]{:S(2)}, u32[]{:S(2)}) %all-to-all-start) | async-done | bytes 1114144 | tf_op jit(solution)/shard_map/all_to_all | solution.py:183
  79.2 0.7 slice_convert_fusion
  79.8 0.4 copy-done.1
  80.2 4.2 %shard_map.79 = (f32[16,128,128]{2,1,0:T(8,128)}, f32[16,128,128]{2,1,0:T(8,128)}) custom-call(s32[16,2]{1,0:T(8,128)} %bitcast.15, s32[1]{0:T(128)} %bitcast.5.core, bf16[16,272,128]{2,1,0:T(8,128)(2,1)} %copy-done.1, bf16[8,128,128]{2,1,0:T(8,128)(2,1)} %bitcast.12), custom_call_target="tpu_custom_call" | custom-call | tf_op jit(solution)/shard_map/pallas_call | solution.py:132
  84.4 1.9 %collective-permute-start.3 = (f32[16,128,128]{2,1,0:T(8,128)}, f32[16,128,128]{2,1,0:T(8,128)S(1)}, u32[]{:S(2)}, u32[]{:S(2)}) collective-permute-start(f32[16,128,128]{2,1,0:T(8,128)} %get-tuple-element.9), channel_id=1, source_target_pairs={{0,1},{1,0},{2,3},{3,2},{4,5},{5,4},{6,7},{7,6},{8,9},{9,8},{10,11... | collective-permute-start | bytes 3145736 | tf_op jit(solution)/shard_map/ppermute | solution.py:201
  86.3 2.8 %collective-permute-done.3 = f32[16,128,128]{2,1,0:T(8,128)S(1)} collective-permute-done((f32[16,128,128]{2,1,0:T(8,128)}, f32[16,128,128]{2,1,0:T(8,128)S(1)}, u32[]{:S(2)}, u32[]{:S(2)}) %collective-permute-start.3) | collective-permute-done | bytes 1048608 | tf_op jit(solution)/shard_map/ppermute | solution.py:201
  89.1 1.3 add.10
  90.5 20.2 %all_to_all.15 = f32[16,128,128]{2,1,0:T(8,128)S(1)} all-to-all(f32[16,128,128]{2,1,0:T(8,128)S(1)} %add.10), channel_id=1, replica_groups={{0,2,4,6,8,10,12,14,16,18,20,22,24,26,28,30},{1,3,5,7,9,11,13,15,17,19,..., dimensions={0} | all-to-all | bytes 2097152 | tf_op jit(solution)/shard_map/all_to_all | solution.py:203
  110.7 0.1 reduce_sum.9
  110.8 20.9 %all_to_all.16 = f32[16,8,128]{2,1,0:T(8,128)} all-to-all(f32[16,8,128]{2,1,0:T(8,128)S(1)} %bitcast.13), channel_id=1, replica_groups=mesh['corpus'=16,'frow'=4,'fcol'=8] {'corpus'}, dimensions={0} | all-to-all | bytes 131072 | tf_op jit(solution)/shard_map/all_to_all | solution.py:207
  131.7 1.5 %shard_map.80 = f32[16,4,128]{2,1,0:T(4,128)} custom-call(s32[1,16]{1,0:T(1,128)} %get-tuple-element.6.places, s32[1,16]{1,0:T(1,128)} %trains.3, s32[1]{0:T(128)S(6)} %copy.13.count, f32[32,4,128]{2,1,0:T(4,128)} %bitcast.14, f32[16,128]{1,0:T(8,128)} %bitcast.17), custom_call_target="tpu_custom_call" | custom-call | tf_op jit(solution)/shard_map/pallas_call | solution.py:158
  133.2 8.0 %reduce-scatter.2.cloned.1.call-done = f32[256,128]{1,0:T(8,128)} async-done(((f32[4096,128]{1,0:T(8,128)}), f32[256,128]{1,0:T(8,128)}) %reduce-scatter.2.cloned.1.call-update) | async-done | bytes 131088 | tf_op jit(solution)/shard_map/reduce_scatter | solution.py:193
  (12 shorter events, 0.1 us)
Async XLA Ops:
  7.2 50.2 %all-gather.2.cloned.1.call-start = ((), (), s32[]{:S(2)}) async-start(), calls=%async_computation.4 | async-start | bytes 4718592 | tf_op jit(solution)/shard_map/all_gather | solution.py:186
  11.2 15.4 %copy-start = (bf16[2048,128]{1,0:T(8,128)(2,1)S(1)}, bf16[2048,128]{1,0:T(8,128)(2,1)}, u32[]{:S(2)}) copy-start(bf16[2048,128]{1,0:T(8,128)(2,1)} %refs_0_.1) | copy-start | bytes 1572868
  11.3 67.9 %all-to-all-start = ((bf16[16,272,128]{2,1,0:T(8,128)(2,1)}), bf16[16,272,128]{2,1,0:T(8,128)(2,1)S(1)}, u32[]{:S(2)}, u32[]{:S(2)}) async-start(bf16[16,272,128]{2,1,0:T(8,128)(2,1)} %get-tuple-element.7), calls=%async_computation.1 | async-start | bytes 2228224 | tf_op jit(solution)/shard_map/all_to_all | solution.py:183
  26.6 114.5 %reduce-scatter.2.cloned.1.call-start = ((), (), s32[]{:S(2)}) async-start(), calls=%async_computation.5 | async-start | bytes 2228224 | tf_op jit(solution)/shard_map/reduce_scatter | solution.py:193
  26.7 27.7 %collective-permute-start = (bf16[2048,128]{1,0:T(8,128)(2,1)S(1)}, bf16[2048,128]{1,0:T(8,128)(2,1)S(1)}, u32[]{:S(2)}, u32[]{:S(2)}) collective-permute-start(bf16[2048,128]{1,0:T(8,128)(2,1)S(1)} %copy-done), channel_id=1, source_target_pairs={{8,0},{16,8},{24,16},{0,24},{9,1},{17,9},{25,17},{1,25},{10,2},{18... | collective-permute-start | bytes 1572872 | tf_op jit(solution)/shard_map/ppermute | solution.py:188
  29.4 25.0 %collective-permute-start.1 = (bf16[2048,128]{1,0:T(8,128)(2,1)S(1)}, bf16[2048,128]{1,0:T(8,128)(2,1)S(1)}, u32[]{:S(2)}, u32[]{:S(2)}) collective-permute-start(bf16[2048,128]{1,0:T(8,128)(2,1)S(1)} %copy-done), channel_id=1, source_target_pairs={{16,0},{24,8},{0,16},{8,24},{17,1},{25,9},{1,17},{9,25},{18,2},{26... | collective-permute-start | bytes 1572872 | tf_op jit(solution)/shard_map/ppermute | solution.py:188
  32.4 24.5 %collective-permute-start.2 = (bf16[2048,128]{1,0:T(8,128)(2,1)S(1)}, bf16[2048,128]{1,0:T(8,128)(2,1)S(1)}, u32[]{:S(2)}, u32[]{:S(2)}) collective-permute-start(bf16[2048,128]{1,0:T(8,128)(2,1)S(1)} %copy-done), channel_id=1, source_target_pairs={{24,0},{0,8},{8,16},{16,24},{25,1},{1,9},{9,17},{17,25},{26,2},{2,... | collective-permute-start | bytes 1572872 | tf_op jit(solution)/shard_map/ppermute | solution.py:188
  54.4 3.0 %copy-start.2 = (bf16[2048,128]{1,0:T(8,128)(2,1)}, bf16[2048,128]{1,0:T(8,128)(2,1)S(1)}, u32[]{:S(2)}) copy-start(bf16[2048,128]{1,0:T(8,128)(2,1)S(1)} %collective-permute-done.refs_1_) | copy-start | bytes 1572868
  54.4 3.0 %copy-start.3 = (bf16[2048,128]{1,0:T(8,128)(2,1)}, bf16[2048,128]{1,0:T(8,128)(2,1)S(1)}, u32[]{:S(2)}) copy-start(bf16[2048,128]{1,0:T(8,128)(2,1)S(1)} %collective-permute-done.1.refs_2_) | copy-start | bytes 1572868
  56.9 0.8 copy-start.4
  79.2 1.0 copy-start.1
  84.4 4.8 %collective-permute-start.3 = (f32[16,128,128]{2,1,0:T(8,128)}, f32[16,128,128]{2,1,0:T(8,128)S(1)}, u32[]{:S(2)}, u32[]{:S(2)}) collective-permute-start(f32[16,128,128]{2,1,0:T(8,128)} %get-tuple-element.9), channel_id=1, source_target_pairs={{0,1},{1,0},{2,3},{3,2},{4,5},{5,4},{6,7},{7,6},{8,9},{9,8},{10,11... | collective-permute-start | bytes 3145736 | tf_op jit(solution)/shard_map/ppermute | solution.py:201
Sparse Core Ops, SparseCore 0:
  10.1 47.1 all-gather.1
  64.6 76.5 reduce-scatter.1

commit v4 on v3

--- a/solution.py
+++ b/solution.py
@@ -11,50 +11,56 @@
 PAIRS = 16
 CAP = 2
 CORES = 2
+PAIR = 2
 ID_ROWS = 16
 VMEM_BYTES = 56 * 1024 * 1024
 
 
 def gram_kernel(scale, x_size, place, rows_ref, *refs):
     out_ref = refs[-1]
-    depth, width = rows_ref.shape[1], out_ref.shape[1]
+    slices, _, width = rows_ref.shape
     frow_at, fcol_at, col_groups = place[0], place[1], place[2]
     columns = jnp.concatenate([ref[...] for ref in refs[:-1]], axis=1)
-    product = lax.dot_general(
-        rows_ref[...], columns, (((0,), (0,)), ((), ())), preferred_element_type=jnp.float32
-    )
-    row_first = frow_at * col_groups * width + pl.program_id(0) * depth
+    depth = PAIR * width
     iota = [lax.broadcasted_iota(jnp.int32, (depth, width), axis) for axis in (0, 1)]
-    for c in range(x_size):
-        column_at = lax.rem(frow_at + c, x_size)
-        column_first = (column_at * col_groups + fcol_at) * width
-        keep = row_first + iota[0] <= column_first + iota[1]
-        block = product[:, c * width:(c + 1) * width]
-        out_ref[pl.ds(column_at, depth, stride=x_size), :] = jnp.where(keep, block * scale, 0.0)
-
-
-def gram_tile(rows, columns, place, scale):
+    for at in range(0, slices, PAIR):
+        rows = jnp.concatenate([rows_ref[at + j] for j in range(PAIR)], axis=1)
+        product = lax.dot_general(
+            rows, columns, (((0,), (0,)), ((), ())), preferred_element_type=jnp.float32
+        )
+        row_first = (frow_at * col_groups + pl.program_id(0) * slices + at) * width
+        for c in range(x_size):
+            column_at = lax.rem(frow_at + c, x_size)
+            column_first = (column_at * col_groups + fcol_at) * width
+            keep = row_first + iota[0] <= column_first + iota[1]
+            block = product[:, c * width:(c + 1) * width]
+            out_ref[pl.ds(at * width * x_size + column_at, depth, stride=x_size), :] = jnp.where(
+                keep, block * scale, 0.0
+            )
+
+
+def gram_tile(panel, columns, place, scale):
     depth, width = columns[0].shape
-    x_size, panel = len(columns), rows.shape[1]
-    step = 4 * width
-    shape = (panel * x_size, width)
+    x_size, slices = len(columns), panel.shape[0]
+    step = slices // 2
+    shape = (slices * width * x_size, width)
     return pl.pallas_call(
         functools.partial(gram_kernel, scale, x_size),
         out_shape=jax.ShapeDtypeStruct(shape, jnp.float32),
         grid_spec=pltpu.PrefetchScalarGridSpec(
             num_scalar_prefetch=1,
-            grid=(panel // step,),
-            in_specs=[pl.BlockSpec((depth, step), lambda i, place: (0, i))]
+            grid=(slices // step,),
+            in_specs=[pl.BlockSpec((step, depth, width), lambda i, place: (i, 0, 0))]
             + [pl.BlockSpec((depth, width), lambda i, place: (0, 0))] * x_size,
-            out_specs=pl.BlockSpec((step * x_size, width), lambda i, place: (i, 0)),
+            out_specs=pl.BlockSpec((step * width * x_size, width), lambda i, place: (i, 0)),
         ),
         compiler_params=pltpu.CompilerParams(vmem_limit_bytes=VMEM_BYTES),
         cost_estimate=pl.CostEstimate(
             flops=2 * depth * shape[0] * width,
-            bytes_accessed=2 * depth * (panel + x_size * width) + 4 * shape[0] * width,
+            bytes_accessed=2 * depth * (slices + x_size) * width + 4 * shape[0] * width,
             transcendentals=0,
         ),
-    )(place, rows, *columns)
+    )(place, panel, *columns)
 
 
 def offer_kernel(held, tests, trains, count, trains_ref, out_ref, places, seen, block_of, id_of):
@@ -141,7 +147,7 @@
             ],
             out_specs=[out_block] * 2,
         ),
-        compiler_params=pltpu.CompilerParams(vmem_limit_bytes=VMEM_BYTES),
+        compiler_params=pltpu.CompilerParams(vmem_limit_bytes=16 * 1024 * 1024),
     )(ids, core, offered, tests)
 
 
@@ -183,10 +189,11 @@
     offered = lax.all_to_all(offered, "corpus", 0, 0, tiled=True)
     ids = offered[:, CAP * TB, :CAP].astype(jnp.int32)
 
-    panel = lax.all_gather(feature_slab, "fcol", axis=1, tiled=True)
-    columns = [feature_slab] + [
-        lax.ppermute(feature_slab, "frow", shift("frow", by)) for by in range(1, row_groups)
-    ]
+    panel = lax.all_gather(feature_slab, "fcol")
+    columns = [feature_slab]
+    for by in reversed(range(1, row_groups)):
+        pairs = [(source, to) for source, to in shift("frow", by) if source > to]
+        columns.insert(1, lax.ppermute(feature_slab, "frow", pairs))
     place = jnp.stack([frow_at, fcol_at, jnp.int32(col_groups)]).astype(jnp.int32)
     norm_scale = (slab_rows * corpus_size) ** (-0.5)
     tile = gram_tile(panel, columns, place, norm_scale)

time: 149 us -> 144 us (0.966)
  the two profiles are of different devices: /device:TPU:30 before, /device:TPU:14 now
where the time goes in v4:
time: 144 us
  waiting for transfers between devices  48.6 us (34%)
  blocking collectives  42.5 us (30%)
  starting transfers between devices  24.4 us (17%)
  between operations  14.8 us (10%)
  Pallas kernels  12.3 us (9%)
    all_to_all x1, blocking collectives, shards(): lax.all_to_all(partials, ('frow', 'fcol'), 0, 0, axis_index_groups=same_c...  21.6 us
    all_to_all x1, blocking collectives, shards(): lax.all_to_all(summed.reshape(corpus_size, -1, TB), 'corpus', 0, 0, tiled...  21 us
    all_to_all x1, waiting for transfers between devices, shards(): offered = lax.all_to_all(offered, 'corpus', 0, 0, tiled=True)  18.9 us
    ppermute x3, waiting for transfers between devices, shards(): columns.insert(1, lax.ppermute(feature_slab, 'frow', pairs))  18.4 us
    all_to_all x1, starting transfers between devices, shards(): offered = lax.all_to_all(offered, 'corpus', 0, 0, tiled=True)  15.3 us
    reduce_scatter x1, waiting for transfers between devices, shards(): lax.psum_scatter(tile, 'corpus', scatter_dimension=0, tiled=True)  7.53 us
    ppermute x3, starting transfers between devices, shards(): columns.insert(1, lax.ppermute(feature_slab, 'frow', pairs))  7.11 us
    pallas_call x1, Pallas kernels, gram_tile(): pl.pallas_call(functools.partial(gram_kernel, scale, x_size), out_shape=j...  6.61 us
  transfers between devices with their start and end apart: 7, of which 7 were waited for; matrix products, arithmetic and copies ran while one was open for 1% of the time, Pallas kernels for 9%

profile of v4, /device:TPU:14, one launch (start us, length us, event | category | flops | bytes accessed | tf_op | source)
XLA Modules:
  0.0 143.9 jit_solution(13366190362721012362)
XLA Ops:
  7.2 0.7 all-gather.3.cloned.1.call-update
  8.5 2.7 %shard_map.78 = (bf16[16,272,128]{2,1,0:T(8,128)(2,1)}, s32[1,16]{1,0:T(1,128)}) custom-call(s32[1,16]{1,0:T(1,128)} %tests.1, s32[1,16]{1,0:T(1,128)} %trains.3, s32[1]{0:T(128)S(6)} %copy.13.count, bf16[16,128,128]{2,1,0:T(8,128)(2,1)} %bitcast.14), custom_call_target="tpu_custom_call" | custom-call | tf_op jit(solution)/shard_map/pallas_call | solution.py:101
  11.3 15.3 %all-to-all-start = ((bf16[16,272,128]{2,1,0:T(8,128)(2,1)}), bf16[16,272,128]{2,1,0:T(8,128)(2,1)S(1)}, u32[]{:S(2)}, u32[]{:S(2)}) async-start(bf16[16,272,128]{2,1,0:T(8,128)(2,1)} %get-tuple-element.7), calls=%async_computation.1 | async-start | bytes 2228224 | tf_op jit(solution)/shard_map/all_to_all | solution.py:189
  26.6 0.0 reduce-scatter.2.cloned.1.call-start
  26.7 2.8 %collective-permute-start = (bf16[2048,128]{1,0:T(8,128)(2,1)S(1)}, bf16[2048,128]{1,0:T(8,128)(2,1)S(1)}, u32[]{:S(2)}, u32[]{:S(2)}) collective-permute-start(bf16[2048,128]{1,0:T(8,128)(2,1)S(1)} %copy-done.1), channel_id=1, source_target_pairs={{8,0},{16,8},{24,16},{9,1},{17,9},{25,17},{10,2},{18,10},{26,18},{... | collective-permute-start | bytes 1572872 | tf_op jit(solution)/shard_map/ppermute | solution.py:196
  29.4 3.0 %collective-permute-start.1 = (bf16[2048,128]{1,0:T(8,128)(2,1)S(1)}, bf16[2048,128]{1,0:T(8,128)(2,1)S(1)}, u32[]{:S(2)}, u32[]{:S(2)}) collective-permute-start(bf16[2048,128]{1,0:T(8,128)(2,1)S(1)} %copy-done.1), channel_id=1, source_target_pairs={{16,0},{24,8},{17,1},{25,9},{18,2},{26,10},{19,3},{27,11},{20,4},{... | collective-permute-start | bytes 1572872 | tf_op jit(solution)/shard_map/ppermute | solution.py:196
  32.5 1.3 collective-permute-start.2
  33.8 0.6 pad_add_fusion.place
  34.4 7.4 %collective-permute-done.refs_1_ = bf16[2048,128]{1,0:T(8,128)(2,1)S(1)} collective-permute-done((bf16[2048,128]{1,0:T(8,128)(2,1)S(1)}, bf16[2048,128]{1,0:T(8,128)(2,1)S(1)}, u32[]{:S(2)}, u32[]{:S(2)}) %collective-permute-start) | collective-permute-done | bytes 524320 | tf_op jit(solution)/shard_map/ppermute | solution.py:196
  41.8 9.8 %collective-permute-done.1.refs_2_ = bf16[2048,128]{1,0:T(8,128)(2,1)S(1)} collective-permute-done((bf16[2048,128]{1,0:T(8,128)(2,1)S(1)}, bf16[2048,128]{1,0:T(8,128)(2,1)S(1)}, u32[]{:S(2)}, u32[]{:S(2)}) %collective-permute-start.1) | collective-permute-done | bytes 524320 | tf_op jit(solution)/shard_map/ppermute | solution.py:196
  51.5 1.3 collective-permute-done.2.refs_3_
  52.8 0.5 all-gather.3.cloned.1.call-done
  53.3 0.4 copy-done.4
  53.6 6.6 %shard_map.77 = f32[4096,128]{1,0:T(8,128)} custom-call(s32[3]{0:T(128)} %pad_add_fusion.place, bf16[8,2048,128]{2,1,0:T(8,128)(2,1)} %bitcast.15, bf16[2048,128]{1,0:T(8,128)(2,1)} %refs_0_.1, bf16[2048,128]{1,0:T(8,128)(2,1)} %copy-done.2, bf16[2048,128]{1,0:T(8,128)(2,1)} %copy-done.3, bf16[2048,128]{1,0:T(8,128)(2,1)} %copy-done.4), custom_call_target="tpu_custom_call" | custom-call | flops 2147483648 | bytes 8388608 | tf_op jit(solution)/shard_map/pallas_call | solution.py:47
  60.3 18.9 %all-to-all-done.offered_ref = bf16[16,272,128]{2,1,0:T(8,128)(2,1)S(1)} async-done(((bf16[16,272,128]{2,1,0:T(8,128)(2,1)}), bf16[16,272,128]{2,1,0:T(8,128)(2,1)S(1)}, u32[]{:S(2)}, u32[]{:S(2)}) %all-to-all-start) | async-done | bytes 1114144 | tf_op jit(solution)/shard_map/all_to_all | solution.py:189
  79.2 1.5 %shard_map.79 = (f32[16,128,128]{2,1,0:T(8,128)S(1)}, f32[16,128,128]{2,1,0:T(8,128)S(1)}) custom-call(s32[16,2]{1,0:T(8,128)S(1)} %bitcast.13, s32[1]{0:T(128)} %bitcast.6.core, bf16[16,272,128]{2,1,0:T(8,128)(2,1)S(1)} %all-to-all-done.offered_ref, bf16[8,128,128]{2,1,0:T(8,128)(2,1)S(1)} %bitcast.12), custom_call_target="tpu_custom_call" | custom-call | tf_op jit(solution)/shard_map/pallas_call | solution.py:138
  80.7 1.9 %collective-permute-start.3 = (f32[16,128,128]{2,1,0:T(8,128)S(1)}, f32[16,128,128]{2,1,0:T(8,128)S(1)}, u32[]{:S(2)}, u32[]{:S(2)}) collective-permute-start(f32[16,128,128]{2,1,0:T(8,128)S(1)} %get-tuple-element.9), channel_id=1, source_target_pairs={{0,1},{1,0},{2,3},{3,2},{4,5},{5,4},{6,7},{7,6},{8,9},{9,8},{10,11... | collective-permute-start | bytes 3145736 | tf_op jit(solution)/shard_map/ppermute | solution.py:208
  82.6 2.6 %collective-permute-done.3 = f32[16,128,128]{2,1,0:T(8,128)S(1)} collective-permute-done((f32[16,128,128]{2,1,0:T(8,128)S(1)}, f32[16,128,128]{2,1,0:T(8,128)S(1)}, u32[]{:S(2)}, u32[]{:S(2)}) %collective-permute-start.3) | collective-permute-done | bytes 1048608 | tf_op jit(solution)/shard_map/ppermute | solution.py:208
  85.3 0.1 add.10
  85.4 21.6 %all_to_all.15 = f32[16,128,128]{2,1,0:T(8,128)S(1)} all-to-all(f32[16,128,128]{2,1,0:T(8,128)S(1)} %add.10), channel_id=1, replica_groups={{0,2,4,6,8,10,12,14,16,18,20,22,24,26,28,30},{1,3,5,7,9,11,13,15,17,19,..., dimensions={0} | all-to-all | bytes 2097152 | tf_op jit(solution)/shard_map/all_to_all | solution.py:210
  107.0 0.1 reduce_sum.9
  107.0 21.0 %all_to_all.16 = f32[16,8,128]{2,1,0:T(8,128)} all-to-all(f32[16,8,128]{2,1,0:T(8,128)S(1)} %bitcast.16), channel_id=1, replica_groups=mesh['corpus'=16,'frow'=4,'fcol'=8] {'corpus'}, dimensions={0} | all-to-all | bytes 131072 | tf_op jit(solution)/shard_map/all_to_all | solution.py:214
  128.0 1.5 %shard_map.80 = f32[16,4,128]{2,1,0:T(4,128)} custom-call(s32[1,16]{1,0:T(1,128)} %get-tuple-element.6.places, s32[1,16]{1,0:T(1,128)} %trains.3, s32[1]{0:T(128)S(6)} %copy.13.count, f32[32,4,128]{2,1,0:T(4,128)} %bitcast.17, f32[16,128]{1,0:T(8,128)} %bitcast.19), custom_call_target="tpu_custom_call" | custom-call | tf_op jit(solution)/shard_map/pallas_call | solution.py:164
  129.5 7.5 %reduce-scatter.2.cloned.1.call-done = f32[256,128]{1,0:T(8,128)} async-done(((f32[4096,128]{1,0:T(8,128)}), f32[256,128]{1,0:T(8,128)}) %reduce-scatter.2.cloned.1.call-update) | async-done | bytes 131088 | tf_op jit(solution)/shard_map/reduce_scatter | solution.py:200
  (12 shorter events, 0.1 us)
Async XLA Ops:
  7.2 46.1 %all-gather.3.cloned.1.call-start = ((), (), s32[]{:S(2)}) async-start(), calls=%async_computation.5 | async-start | bytes 4718592 | tf_op jit(solution)/shard_map/all_gather | solution.py:192
  11.2 15.4 %copy-start.1 = (bf16[2048,128]{1,0:T(8,128)(2,1)S(1)}, bf16[2048,128]{1,0:T(8,128)(2,1)}, u32[]{:S(2)}) copy-start(bf16[2048,128]{1,0:T(8,128)(2,1)} %refs_0_.1) | copy-start | bytes 1572868
  11.3 67.9 %all-to-all-start = ((bf16[16,272,128]{2,1,0:T(8,128)(2,1)}), bf16[16,272,128]{2,1,0:T(8,128)(2,1)S(1)}, u32[]{:S(2)}, u32[]{:S(2)}) async-start(bf16[16,272,128]{2,1,0:T(8,128)(2,1)} %get-tuple-element.7), calls=%async_computation.1 | async-start | bytes 2228224 | tf_op jit(solution)/shard_map/all_to_all | solution.py:189
  26.6 110.4 %reduce-scatter.2.cloned.1.call-start = ((), (), s32[]{:S(2)}) async-start(), calls=%async_computation.4 | async-start | bytes 2228224 | tf_op jit(solution)/shard_map/reduce_scatter | solution.py:200
  26.7 15.1 %collective-permute-start = (bf16[2048,128]{1,0:T(8,128)(2,1)S(1)}, bf16[2048,128]{1,0:T(8,128)(2,1)S(1)}, u32[]{:S(2)}, u32[]{:S(2)}) collective-permute-start(bf16[2048,128]{1,0:T(8,128)(2,1)S(1)} %copy-done.1), channel_id=1, source_target_pairs={{8,0},{16,8},{24,16},{9,1},{17,9},{25,17},{10,2},{18,10},{26,18},{... | collective-permute-start | bytes 1572872 | tf_op jit(solution)/shard_map/ppermute | solution.py:196
  29.4 22.1 %collective-permute-start.1 = (bf16[2048,128]{1,0:T(8,128)(2,1)S(1)}, bf16[2048,128]{1,0:T(8,128)(2,1)S(1)}, u32[]{:S(2)}, u32[]{:S(2)}) collective-permute-start(bf16[2048,128]{1,0:T(8,128)(2,1)S(1)} %copy-done.1), channel_id=1, source_target_pairs={{16,0},{24,8},{17,1},{25,9},{18,2},{26,10},{19,3},{27,11},{20,4},{... | collective-permute-start | bytes 1572872 | tf_op jit(solution)/shard_map/ppermute | solution.py:196
  32.5 20.3 %collective-permute-start.2 = (bf16[2048,128]{1,0:T(8,128)(2,1)S(1)}, bf16[2048,128]{1,0:T(8,128)(2,1)S(1)}, u32[]{:S(2)}, u32[]{:S(2)}) collective-permute-start(bf16[2048,128]{1,0:T(8,128)(2,1)S(1)} %copy-done.1), channel_id=1, source_target_pairs={{24,0},{25,1},{26,2},{27,3},{28,4},{29,5},{30,6},{31,7},{56,32},{5... | collective-permute-start | bytes 1572872 | tf_op jit(solution)/shard_map/ppermute | solution.py:196
  41.8 11.5 %copy-start.2 = (bf16[2048,128]{1,0:T(8,128)(2,1)}, bf16[2048,128]{1,0:T(8,128)(2,1)S(1)}, u32[]{:S(2)}) copy-start(bf16[2048,128]{1,0:T(8,128)(2,1)S(1)} %collective-permute-done.refs_1_) | copy-start | bytes 1572868
  51.5 1.8 %copy-start.3 = (bf16[2048,128]{1,0:T(8,128)(2,1)}, bf16[2048,128]{1,0:T(8,128)(2,1)S(1)}, u32[]{:S(2)}) copy-start(bf16[2048,128]{1,0:T(8,128)(2,1)S(1)} %collective-permute-done.1.refs_2_) | copy-start | bytes 1572868
  52.8 0.8 copy-start.4
  60.3 18.9 %copy-start = (bf16[1024,128]{1,0:T(8,128)(2,1)S(1)}, bf16[1024,128]{1,0:T(8,128)(2,1)}, u32[]{:S(2)}) copy-start(bf16[1024,128]{1,0:T(8,128)(2,1)} %param.7) | copy-start | bytes 786436
  80.7 4.6 %collective-permute-start.3 = (f32[16,128,128]{2,1,0:T(8,128)S(1)}, f32[16,128,128]{2,1,0:T(8,128)S(1)}, u32[]{:S(2)}, u32[]{:S(2)}) collective-permute-start(f32[16,128,128]{2,1,0:T(8,128)S(1)} %get-tuple-element.9), channel_id=1, source_target_pairs={{0,1},{1,0},{2,3},{3,2},{4,5},{5,4},{6,7},{7,6},{8,9},{9,8},{10,11... | collective-permute-start | bytes 3145736 | tf_op jit(solution)/shard_map/ppermute | solution.py:208
Sparse Core Ops, SparseCore 0:
  10.1 43.0 all-gather.2
  60.4 76.5 reduce-scatter.1

commit v5 on v4

--- a/solution.py
+++ b/solution.py
@@ -16,45 +16,60 @@
 VMEM_BYTES = 56 * 1024 * 1024
 
 
-def gram_kernel(scale, x_size, place, rows_ref, *refs):
-    out_ref = refs[-1]
-    slices, _, width = rows_ref.shape
+def gram_kernel(scale, x_size, place, panel_ref, *refs):
+    out_ref, held, tile, arrived, left = refs[-5:]
+    slices, _, width = held.shape
     frow_at, fcol_at, col_groups = place[0], place[1], place[2]
-    columns = jnp.concatenate([ref[...] for ref in refs[:-1]], axis=1)
+    arrivals = [
+        pltpu.make_async_copy(panel_ref.at[at], held.at[at], arrived.at[at]) for at in range(slices)
+    ]
+    for copy in arrivals:
+        copy.start()
+    columns = jnp.concatenate([ref[...] for ref in refs[:-5]], axis=1)
     depth = PAIR * width
     iota = [lax.broadcasted_iota(jnp.int32, (depth, width), axis) for axis in (0, 1)]
+    leaving = []
     for at in range(0, slices, PAIR):
-        rows = jnp.concatenate([rows_ref[at + j] for j in range(PAIR)], axis=1)
+        for copy in arrivals[at:at + PAIR]:
+            copy.wait()
+        rows = jnp.concatenate([held[at + j] for j in range(PAIR)], axis=1)
         product = lax.dot_general(
             rows, columns, (((0,), (0,)), ((), ())), preferred_element_type=jnp.float32
         )
-        row_first = (frow_at * col_groups + pl.program_id(0) * slices + at) * width
+        row_first = (frow_at * col_groups + at) * width
         for c in range(x_size):
             column_at = lax.rem(frow_at + c, x_size)
             column_first = (column_at * col_groups + fcol_at) * width
             keep = row_first + iota[0] <= column_first + iota[1]
             block = product[:, c * width:(c + 1) * width]
-            out_ref[pl.ds(at * width * x_size + column_at, depth, stride=x_size), :] = jnp.where(
+            tile[pl.ds(at * width * x_size + column_at, depth, stride=x_size), :] = jnp.where(
                 keep, block * scale, 0.0
             )
+        done = pl.ds(at * width * x_size, depth * x_size)
+        leaving.append(pltpu.make_async_copy(tile.at[done], out_ref.at[done], left.at[at // PAIR]))
+        leaving[-1].start()
+    for copy in leaving:
+        copy.wait()
 
 
 def gram_tile(panel, columns, place, scale):
     depth, width = columns[0].shape
     x_size, slices = len(columns), panel.shape[0]
-    step = slices // 2
     shape = (slices * width * x_size, width)
+    hbm = pl.BlockSpec(memory_space=pltpu.HBM)
     return pl.pallas_call(
         functools.partial(gram_kernel, scale, x_size),
         out_shape=jax.ShapeDtypeStruct(shape, jnp.float32),
-        grid_spec=pltpu.PrefetchScalarGridSpec(
-            num_scalar_prefetch=1,
-            grid=(slices // step,),
-            in_specs=[pl.BlockSpec((step, depth, width), lambda i, place: (i, 0, 0))]
-            + [pl.BlockSpec((depth, width), lambda i, place: (0, 0))] * x_size,
-            out_specs=pl.BlockSpec((step * width * x_size, width), lambda i, place: (i, 0)),
-        ),
-        compiler_params=pltpu.CompilerParams(vmem_limit_bytes=VMEM_BYTES),
+        in_specs=[pl.BlockSpec(memory_space=pltpu.SMEM), hbm]
+        + [pl.BlockSpec(memory_space=pltpu.VMEM)] * x_size,
+        out_specs=hbm,
+        scratch_shapes=[
+            pltpu.VMEM(panel.shape, panel.dtype),
+            pltpu.VMEM(shape, jnp.float32),
+            pltpu.SemaphoreType.DMA((slices,)),
+            pltpu.SemaphoreType.DMA((slices // PAIR,)),
+        ],
+        compiler_params=pltpu.CompilerParams(vmem_limit_bytes=48 * 1024 * 1024),
         cost_estimate=pl.CostEstimate(
             flops=2 * depth * shape[0] * width,
             bytes_accessed=2 * depth * (slices + x_size) * width + 4 * shape[0] * width,

time: 144 us -> 142 us (0.986)
  the two profiles are of different devices: /device:TPU:14 before, /device:TPU:2 now
where the time goes in v5:
time: 142 us; the launch traced here: 141 us
  waiting for transfers between devices  50 us (35%)
  blocking collectives  43.2 us (30%)
  starting transfers between devices  21.8 us (15%)
  between operations  14.8 us (10%)
  Pallas kernels  11.4 us (8%)
    ppermute x3, waiting for transfers between devices, shards(): columns.insert(1, lax.ppermute(feature_slab, 'frow', pairs))  22.9 us
    all_to_all x1, blocking collectives, shards(): lax.all_to_all(partials, ('frow', 'fcol'), 0, 0, axis_index_groups=same_c...  22.4 us
    all_to_all x1, blocking collectives, shards(): lax.all_to_all(summed.reshape(corpus_size, -1, TB), 'corpus', 0, 0, tiled...  20.8 us
    all_to_all x1, waiting for transfers between devices, shards(): offered = lax.all_to_all(offered, 'corpus', 0, 0, tiled=True)  19 us
    all_to_all x1, starting transfers between devices, shards(): offered = lax.all_to_all(offered, 'corpus', 0, 0, tiled=True)  15.3 us
    pallas_call x1, Pallas kernels, gram_tile(): pl.pallas_call(functools.partial(gram_kernel, scale, x_size), out_shape=j...  5.62 us
    ppermute x3, starting transfers between devices, shards(): columns.insert(1, lax.ppermute(feature_slab, 'frow', pairs))  4.43 us
    reduce_scatter x1, waiting for transfers between devices, shards(): lax.psum_scatter(tile, 'corpus', scatter_dimension=0, tiled=True)  4.41 us
  transfers between devices with their start and end apart: 7, of which 6 were waited for; matrix products, arithmetic and copies ran while one was open for 0% of the time, Pallas kernels for 8%

profile of v5, /device:TPU:2, one launch (start us, length us, event | category | flops | bytes accessed | tf_op | source)
XLA Modules:
  0.0 141.4 jit_solution(2398795691043734717)
XLA Ops:
  7.2 0.0 all-gather.3.cloned.1.call-start
  7.2 0.7 all-gather.3.cloned.1.call-update
  8.5 2.7 %shard_map.78 = (bf16[16,272,128]{2,1,0:T(8,128)(2,1)}, s32[1,16]{1,0:T(1,128)}) custom-call(s32[1,16]{1,0:T(1,128)} %tests.1, s32[1,16]{1,0:T(1,128)} %trains.3, s32[1]{0:T(128)S(6)} %copy.13.count, bf16[16,128,128]{2,1,0:T(8,128)(2,1)} %bitcast.12), custom_call_target="tpu_custom_call" | custom-call | tf_op jit(solution)/shard_map/pallas_call | solution.py:116
  11.3 15.3 %all-to-all-start = ((bf16[16,272,128]{2,1,0:T(8,128)(2,1)}), bf16[16,272,128]{2,1,0:T(8,128)(2,1)S(1)}, u32[]{:S(2)}, u32[]{:S(2)}) async-start(bf16[16,272,128]{2,1,0:T(8,128)(2,1)} %get-tuple-element.7), calls=%async_computation.1 | async-start | bytes 2228224 | tf_op jit(solution)/shard_map/all_to_all | solution.py:204
  26.6 0.0 reduce-scatter.2.cloned.1.call-start
  26.7 2.4 %collective-permute-start = (bf16[2048,128]{1,0:T(8,128)(2,1)S(1)}, bf16[2048,128]{1,0:T(8,128)(2,1)S(1)}, u32[]{:S(2)}, u32[]{:S(2)}) collective-permute-start(bf16[2048,128]{1,0:T(8,128)(2,1)S(1)} %copy-done), channel_id=1, source_target_pairs={{8,0},{16,8},{24,16},{9,1},{17,9},{25,17},{10,2},{18,10},{26,18},{... | collective-permute-start | bytes 1572872 | tf_op jit(solution)/shard_map/ppermute | solution.py:211
  29.1 1.3 collective-permute-start.1
  30.4 0.7 collective-permute-start.2
  31.1 0.1 pad_add_fusion.place
  31.2 11.3 %collective-permute-done.refs_1_ = bf16[2048,128]{1,0:T(8,128)(2,1)S(1)} collective-permute-done((bf16[2048,128]{1,0:T(8,128)(2,1)S(1)}, bf16[2048,128]{1,0:T(8,128)(2,1)S(1)}, u32[]{:S(2)}, u32[]{:S(2)}) %collective-permute-start) | collective-permute-done | bytes 524320 | tf_op jit(solution)/shard_map/ppermute | solution.py:211
  42.5 11.6 %collective-permute-done.1.refs_2_ = bf16[2048,128]{1,0:T(8,128)(2,1)S(1)} collective-permute-done((bf16[2048,128]{1,0:T(8,128)(2,1)S(1)}, bf16[2048,128]{1,0:T(8,128)(2,1)S(1)}, u32[]{:S(2)}, u32[]{:S(2)}) %collective-permute-start.1) | collective-permute-done | bytes 524320 | tf_op jit(solution)/shard_map/ppermute | solution.py:211
  54.1 0.3 all-gather.3.cloned.1.call-done
  54.4 5.6 %shard_map.77 = f32[4096,128]{1,0:T(8,128)} custom-call(s32[3]{0:T(128)S(1)} %pad_add_fusion.place, bf16[8,2048,128]{2,1,0:T(8,128)(2,1)} %bitcast.15, bf16[2048,128]{1,0:T(8,128)(2,1)S(1)} %copy-done, bf16[2048,128]{1,0:T(8,128)(2,1)S(1)} %collective-permute-done.refs_1_, bf16[2048,128]{1,0:T(8,128)(2,1)S(1)} %collective-permute-done.1.refs_2_, ...), custom_call_target="tpu_custom_call" | custom-call | flops 2147483648 | bytes 8388608 | tf_op jit(solution)/shard_map/pallas_call | solution.py:60
  60.1 0.0 reduce-scatter.2.cloned.1.call-update
  60.1 19.0 %all-to-all-done.offered_ref = bf16[16,272,128]{2,1,0:T(8,128)(2,1)S(1)} async-done(((bf16[16,272,128]{2,1,0:T(8,128)(2,1)}), bf16[16,272,128]{2,1,0:T(8,128)(2,1)S(1)}, u32[]{:S(2)}, u32[]{:S(2)}) %all-to-all-start) | async-done | bytes 1114144 | tf_op jit(solution)/shard_map/all_to_all | solution.py:204
  79.2 1.5 %shard_map.79 = (f32[16,128,128]{2,1,0:T(8,128)S(1)}, f32[16,128,128]{2,1,0:T(8,128)S(1)}) custom-call(s32[16,2]{1,0:T(8,128)S(1)} %bitcast.14, s32[1]{0:T(128)} %bitcast.6.core, bf16[16,272,128]{2,1,0:T(8,128)(2,1)S(1)} %all-to-all-done.offered_ref, bf16[8,128,128]{2,1,0:T(8,128)(2,1)S(1)} %bitcast.13), custom_call_target="tpu_custom_call" | custom-call | tf_op jit(solution)/shard_map/pallas_call | solution.py:153
  80.7 1.9 %collective-permute-start.3 = (f32[16,128,128]{2,1,0:T(8,128)S(1)}, f32[16,128,128]{2,1,0:T(8,128)S(1)}, u32[]{:S(2)}, u32[]{:S(2)}) collective-permute-start(f32[16,128,128]{2,1,0:T(8,128)S(1)} %get-tuple-element.9), channel_id=1, source_target_pairs={{0,1},{1,0},{2,3},{3,2},{4,5},{5,4},{6,7},{7,6},{8,9},{9,8},{10,11... | collective-permute-start | bytes 3145736 | tf_op jit(solution)/shard_map/ppermute | solution.py:223
  82.6 2.6 %collective-permute-done.3 = f32[16,128,128]{2,1,0:T(8,128)S(1)} collective-permute-done((f32[16,128,128]{2,1,0:T(8,128)S(1)}, f32[16,128,128]{2,1,0:T(8,128)S(1)}, u32[]{:S(2)}, u32[]{:S(2)}) %collective-permute-start.3) | collective-permute-done | bytes 1048608 | tf_op jit(solution)/shard_map/ppermute | solution.py:223
  85.3 0.1 add.10
  85.4 22.4 %all_to_all.15 = f32[16,128,128]{2,1,0:T(8,128)S(1)} all-to-all(f32[16,128,128]{2,1,0:T(8,128)S(1)} %add.10), channel_id=1, replica_groups={{0,2,4,6,8,10,12,14,16,18,20,22,24,26,28,30},{1,3,5,7,9,11,13,15,17,19,..., dimensions={0} | all-to-all | bytes 2097152 | tf_op jit(solution)/shard_map/all_to_all | solution.py:225
  107.8 0.1 reduce_sum.9
  107.9 20.8 %all_to_all.16 = f32[16,8,128]{2,1,0:T(8,128)} all-to-all(f32[16,8,128]{2,1,0:T(8,128)S(1)} %bitcast.16), channel_id=1, replica_groups=mesh['corpus'=16,'frow'=4,'fcol'=8] {'corpus'}, dimensions={0} | all-to-all | bytes 131072 | tf_op jit(solution)/shard_map/all_to_all | solution.py:229
  128.7 1.5 %shard_map.80 = f32[16,4,128]{2,1,0:T(4,128)} custom-call(s32[1,16]{1,0:T(1,128)} %get-tuple-element.6.places, s32[1,16]{1,0:T(1,128)} %trains.3, s32[1]{0:T(128)S(6)} %copy.13.count, f32[32,4,128]{2,1,0:T(4,128)} %bitcast.17, f32[16,128]{1,0:T(8,128)} %bitcast.19), custom_call_target="tpu_custom_call" | custom-call | tf_op jit(solution)/shard_map/pallas_call | solution.py:179
  130.2 4.4 %reduce-scatter.2.cloned.1.call-done = f32[256,128]{1,0:T(8,128)} async-done(((f32[4096,128]{1,0:T(8,128)}), f32[256,128]{1,0:T(8,128)}) %reduce-scatter.2.cloned.1.call-update) | async-done | bytes 131088 | tf_op jit(solution)/shard_map/reduce_scatter | solution.py:215
  (6 shorter events, 0.0 us)
Async XLA Ops:
  7.2 47.3 %all-gather.3.cloned.1.call-start = ((), (), s32[]{:S(2)}) async-start(), calls=%async_computation.5 | async-start | bytes 4718592 | tf_op jit(solution)/shard_map/all_gather | solution.py:207
  11.3 15.4 %copy-start = (bf16[2048,128]{1,0:T(8,128)(2,1)S(1)}, bf16[2048,128]{1,0:T(8,128)(2,1)}, u32[]{:S(2)}) copy-start(bf16[2048,128]{1,0:T(8,128)(2,1)} %refs_0_.1) | copy-start | bytes 1572868
  11.3 67.9 %all-to-all-start = ((bf16[16,272,128]{2,1,0:T(8,128)(2,1)}), bf16[16,272,128]{2,1,0:T(8,128)(2,1)S(1)}, u32[]{:S(2)}, u32[]{:S(2)}) async-start(bf16[16,272,128]{2,1,0:T(8,128)(2,1)} %get-tuple-element.7), calls=%async_computation.1 | async-start | bytes 2228224 | tf_op jit(solution)/shard_map/all_to_all | solution.py:204
  26.6 108.0 %reduce-scatter.2.cloned.1.call-start = ((), (), s32[]{:S(2)}) async-start(), calls=%async_computation.4 | async-start | bytes 2228224 | tf_op jit(solution)/shard_map/reduce_scatter | solution.py:215
  26.7 15.8 %collective-permute-start = (bf16[2048,128]{1,0:T(8,128)(2,1)S(1)}, bf16[2048,128]{1,0:T(8,128)(2,1)S(1)}, u32[]{:S(2)}, u32[]{:S(2)}) collective-permute-start(bf16[2048,128]{1,0:T(8,128)(2,1)S(1)} %copy-done), channel_id=1, source_target_pairs={{8,0},{16,8},{24,16},{9,1},{17,9},{25,17},{10,2},{18,10},{26,18},{... | collective-permute-start | bytes 1572872 | tf_op jit(solution)/shard_map/ppermute | solution.py:211
  29.1 25.0 %collective-permute-start.1 = (bf16[2048,128]{1,0:T(8,128)(2,1)S(1)}, bf16[2048,128]{1,0:T(8,128)(2,1)S(1)}, u32[]{:S(2)}, u32[]{:S(2)}) collective-permute-start(bf16[2048,128]{1,0:T(8,128)(2,1)S(1)} %copy-done), channel_id=1, source_target_pairs={{16,0},{24,8},{17,1},{25,9},{18,2},{26,10},{19,3},{27,11},{20,4},{... | collective-permute-start | bytes 1572872 | tf_op jit(solution)/shard_map/ppermute | solution.py:211
  30.4 23.7 %collective-permute-start.2 = (bf16[2048,128]{1,0:T(8,128)(2,1)S(1)}, bf16[2048,128]{1,0:T(8,128)(2,1)S(1)}, u32[]{:S(2)}, u32[]{:S(2)}) collective-permute-start(bf16[2048,128]{1,0:T(8,128)(2,1)S(1)} %copy-done), channel_id=1, source_target_pairs={{24,0},{25,1},{26,2},{27,3},{28,4},{29,5},{30,6},{31,7},{56,32},{5... | collective-permute-start | bytes 1572872 | tf_op jit(solution)/shard_map/ppermute | solution.py:211
  60.1 19.1 %copy-start.1 = (bf16[1024,128]{1,0:T(8,128)(2,1)S(1)}, bf16[1024,128]{1,0:T(8,128)(2,1)}, u32[]{:S(2)}) copy-start(bf16[1024,128]{1,0:T(8,128)(2,1)} %param.7) | copy-start | bytes 786436
  80.7 4.6 %collective-permute-start.3 = (f32[16,128,128]{2,1,0:T(8,128)S(1)}, f32[16,128,128]{2,1,0:T(8,128)S(1)}, u32[]{:S(2)}, u32[]{:S(2)}) collective-permute-start(f32[16,128,128]{2,1,0:T(8,128)S(1)} %get-tuple-element.9), channel_id=1, source_target_pairs={{0,1},{1,0},{2,3},{3,2},{4,5},{5,4},{6,7},{7,6},{8,9},{9,8},{10,11... | collective-permute-start | bytes 3145736 | tf_op jit(solution)/shard_map/ppermute | solution.py:223
Sparse Core Ops, SparseCore 0:
  10.1 44.2 all-gather.2
  60.2 74.2 reduce-scatter.1

commit v6 on v5

--- a/solution.py
+++ b/solution.py
@@ -16,7 +16,7 @@
 VMEM_BYTES = 56 * 1024 * 1024
 
 
-def gram_kernel(scale, x_size, place, panel_ref, *refs):
+def gram_kernel(scale, x_size, cuts, place, panel_ref, *refs):
     out_ref, held, tile, arrived, left = refs[-5:]
     slices, _, width = held.shape
     frow_at, fcol_at, col_groups = place[0], place[1], place[2]
@@ -25,7 +25,10 @@
     ]
     for copy in arrivals:
         copy.start()
-    columns = jnp.concatenate([ref[...] for ref in refs[:-5]], axis=1)
+    parts, strips = iter(refs[:-5]), []
+    for count in cuts:
+        strips.append(jnp.concatenate([next(parts)[...] for _ in range(count)], axis=0))
+    columns = jnp.concatenate(strips, axis=1)
     depth = PAIR * width
     iota = [lax.broadcasted_iota(jnp.int32, (depth, width), axis) for axis in (0, 1)]
     leaving = []
@@ -53,15 +56,16 @@
 
 
 def gram_tile(panel, columns, place, scale):
-    depth, width = columns[0].shape
+    depth, width = columns[0][0].shape
     x_size, slices = len(columns), panel.shape[0]
+    cuts = tuple(len(strip) for strip in columns)
     shape = (slices * width * x_size, width)
     hbm = pl.BlockSpec(memory_space=pltpu.HBM)
     return pl.pallas_call(
-        functools.partial(gram_kernel, scale, x_size),
+        functools.partial(gram_kernel, scale, x_size, cuts),
         out_shape=jax.ShapeDtypeStruct(shape, jnp.float32),
         in_specs=[pl.BlockSpec(memory_space=pltpu.SMEM), hbm]
-        + [pl.BlockSpec(memory_space=pltpu.VMEM)] * x_size,
+        + [pl.BlockSpec(memory_space=pltpu.VMEM)] * sum(cuts),
         out_specs=hbm,
         scratch_shapes=[
             pltpu.VMEM(panel.shape, panel.dtype),
@@ -75,38 +79,33 @@
             bytes_accessed=2 * depth * (slices + x_size) * width + 4 * shape[0] * width,
             transcendentals=0,
         ),
-    )(place, panel, *columns)
+    )(place, panel, *[part for strip in columns for part in strip])
 
 
 def offer_kernel(held, tests, trains, count, trains_ref, out_ref, places, seen, block_of, id_of):
     holders = out_ref.shape[0]
+    shift_by = held.bit_length() - 1
+    live = count[0]
+    for h in range(holders + 1):
+        seen[h] = 0
+    for at in range(holders * CAP):
+        block_of[at] = 0
+        id_of[at] = 0
+    for slot in range(PAIRS):
+        test = tests[0, slot]
+        holder = jnp.where(slot < live, lax.shift_right_logical(test, shift_by), holders)
+        rank = seen[holder]
+        seen[holder] = rank + 1
+        place = holder * CAP + rank
+        block_of[place] = trains[0, slot]
+        id_of[place] = lax.bitwise_and(test, held - 1)
+        places[0, slot] = jnp.where(slot < live, place, 0)
     lane = lax.broadcasted_iota(jnp.int32, (ID_ROWS, TB), 1)
-
-    @pl.loop(0, holders)
-    def _(h):
-        seen[h] = 0
-        for r in range(CAP):
-            block_of[h, r] = 0
-            id_of[h, r] = 0
-
-    @pl.loop(0, PAIRS)
-    def _(slot):
-        places[0, slot] = 0
-
-        @pl.when(slot < count[0])
-        def _():
-            holder = tests[0, slot] // held
-            rank = seen[holder]
-            block_of[holder, rank] = trains[0, slot]
-            id_of[holder, rank] = tests[0, slot] - holder * held
-            places[0, slot] = holder * CAP + rank
-            seen[holder] = rank + 1
-
     for h in range(holders):
         ids = jnp.zeros((ID_ROWS, TB), jnp.int32)
         for r in range(CAP):
-            out_ref[h, r * TB:(r + 1) * TB, :] = trains_ref[block_of[h, r]]
-            ids = jnp.where(lane == r, id_of[h, r], ids)
+            out_ref[h, r * TB:(r + 1) * TB, :] = trains_ref[block_of[h * CAP + r]]
+            ids = jnp.where(lane == r, id_of[h * CAP + r], ids)
         out_ref[h, CAP * TB:, :] = ids.astype(jnp.float32).astype(out_ref.dtype)
 
 
@@ -121,8 +120,8 @@
         ),
         in_specs=[smem] * 3 + [pl.BlockSpec(memory_space=pltpu.VMEM)],
         out_specs=(pl.BlockSpec(memory_space=pltpu.VMEM), smem),
-        scratch_shapes=[pltpu.SMEM((holders,), jnp.int32)]
-        + [pltpu.SMEM((holders, CAP), jnp.int32)] * 2,
+        scratch_shapes=[pltpu.SMEM((holders + 1,), jnp.int32)]
+        + [pltpu.SMEM((holders * CAP + PAIRS,), jnp.int32)] * 2,
     )(pair_tests, pair_trains, pair_counts, trains)
 
 
@@ -198,6 +197,7 @@
     fcol_at = lax.axis_index("fcol")
 
     held = test_preconditioned.shape[0] // TB
+    assert held & (held - 1) == 0
     offered, places = offers(
         feature_slab.reshape(-1, TB, feat_width), pair_tests, pair_trains, pair_counts, corpus_size, held
     )
@@ -205,10 +205,18 @@
     ids = offered[:, CAP * TB, :CAP].astype(jnp.int32)
 
     panel = lax.all_gather(feature_slab, "fcol")
-    columns = [feature_slab]
-    for by in reversed(range(1, row_groups)):
+    half = slab_rows // 2
+
+    def down(rows, by):
         pairs = [(source, to) for source, to in shift("frow", by) if source > to]
-        columns.insert(1, lax.ppermute(feature_slab, "frow", pairs))
+        return lax.ppermute(rows, "frow", pairs)
+
+    columns = [[feature_slab], [down(feature_slab, 1)]]
+    for by in range(2, row_groups):
+        if by == 2 < row_groups - 1:
+            columns.append([down(feature_slab[:half], by), down(columns[1][0][half:], 1)])
+        else:
+            columns.append([down(feature_slab, by)])
     place = jnp.stack([frow_at, fcol_at, jnp.int32(col_groups)]).astype(jnp.int32)
     norm_scale = (slab_rows * corpus_size) ** (-0.5)
     tile = gram_tile(panel, columns, place, norm_scale)

time: 142 us -> 142 us (level)
  waiting for transfers between devices: 50 us -> 47 us
  starting transfers between devices: 21.8 us -> 23.7 us
    ppermute x3 -> x4, waiting for transfers between devices: 22.9 us -> 20.2 us  [down(): return lax.ppermute(rows, 'frow', pairs)]
    ppermute x3 -> x4, starting transfers between devices: 4.43 us -> 6.34 us  [down(): return lax.ppermute(rows, 'frow', pairs)]
  transfers between devices with their start and end apart: 7 -> 8, of which waited for: 6 -> 7; matrix products, arithmetic and copies ran while one was open for 0% -> 1% of each run, Pallas kernels for 8% -> 8%
where the time goes in v6:
time: 142 us; the launch traced here: 141 us
  waiting for transfers between devices  47 us (33%)
  blocking collectives  43.8 us (31%)
  starting transfers between devices  23.7 us (17%)
  between operations  14.8 us (10%)
  Pallas kernels  10.9 us (8%)
    all_to_all x1, blocking collectives, shards(): lax.all_to_all(partials, ('frow', 'fcol'), 0, 0, axis_index_groups=same_c...  22.4 us
    all_to_all x1, blocking collectives, shards(): lax.all_to_all(summed.reshape(corpus_size, -1, TB), 'corpus', 0, 0, tiled...  21.4 us
    ppermute x4, waiting for transfers between devices, down(): return lax.ppermute(rows, 'frow', pairs)  20.2 us
    all_to_all x1, waiting for transfers between devices, shards(): offered = lax.all_to_all(offered, 'corpus', 0, 0, tiled=True)  18.7 us
    all_to_all x1, starting transfers between devices, shards(): offered = lax.all_to_all(offered, 'corpus', 0, 0, tiled=True)  15.3 us
    ppermute x4, starting transfers between devices, down(): return lax.ppermute(rows, 'frow', pairs)  6.34 us
    pallas_call x1, Pallas kernels, gram_tile(): pl.pallas_call(functools.partial(gram_kernel, scale, x_size, cuts), out_s...  5.6 us
    reduce_scatter x1, waiting for transfers between devices, shards(): lax.psum_scatter(tile, 'corpus', scatter_dimension=0, tiled=True)  4.05 us
  transfers between devices with their start and end apart: 8, of which 7 were waited for; matrix products, arithmetic and copies ran while one was open for 1% of the time, Pallas kernels for 8%

profile of v6, /device:TPU:2, one launch (start us, length us, event | category | flops | bytes accessed | tf_op | source)
XLA Modules:
  0.0 141.2 jit_solution(16044802073953902667)
XLA Ops:
  7.2 0.7 all-gather.3.cloned.1.call-update
  8.5 2.3 %shard_map.78 = (bf16[16,272,128]{2,1,0:T(8,128)(2,1)}, s32[1,16]{1,0:T(1,128)}) custom-call(s32[1,16]{1,0:T(1,128)} %tests.1, s32[1,16]{1,0:T(1,128)} %trains.3, s32[1]{0:T(128)S(6)} %copy.13.count, bf16[16,128,128]{2,1,0:T(8,128)(2,1)} %bitcast.12), custom_call_target="tpu_custom_call" | custom-call | tf_op jit(solution)/shard_map/pallas_call | solution.py:115
  10.9 15.3 %all-to-all-start = ((bf16[16,272,128]{2,1,0:T(8,128)(2,1)}), bf16[16,272,128]{2,1,0:T(8,128)(2,1)S(1)}, u32[]{:S(2)}, u32[]{:S(2)}) async-start(bf16[16,272,128]{2,1,0:T(8,128)(2,1)} %get-tuple-element.7), calls=%async_computation.1 | async-start | bytes 2228224 | tf_op jit(solution)/shard_map/all_to_all | solution.py:204
  26.3 2.4 %collective-permute-start = (bf16[2048,128]{1,0:T(8,128)(2,1)S(1)}, bf16[2048,128]{1,0:T(8,128)(2,1)S(1)}, u32[]{:S(2)}, u32[]{:S(2)}) collective-permute-start(bf16[2048,128]{1,0:T(8,128)(2,1)S(1)} %copy-done), channel_id=1, source_target_pairs={{8,0},{16,8},{24,16},{9,1},{17,9},{25,17},{10,2},{18,10},{26,18},{... | collective-permute-start | bytes 1572872 | tf_op jit(solution)/shard_map/ppermute | solution.py:212
  28.7 0.7 collective-permute-start.3
  29.4 1.3 collective-permute-start.1
  30.7 11.3 %collective-permute-done.refs_1_ = bf16[2048,128]{1,0:T(8,128)(2,1)S(1)} collective-permute-done((bf16[2048,128]{1,0:T(8,128)(2,1)S(1)}, bf16[2048,128]{1,0:T(8,128)(2,1)S(1)}, u32[]{:S(2)}, u32[]{:S(2)}) %collective-permute-start) | collective-permute-done | bytes 524320 | tf_op jit(solution)/shard_map/ppermute | solution.py:212
  42.1 0.7 slice.12
  42.8 1.9 %collective-permute-start.2 = (bf16[1024,128]{1,0:T(8,128)(2,1)}, bf16[1024,128]{1,0:T(8,128)(2,1)S(1)}, u32[]{:S(2)}, u32[]{:S(2)}) collective-permute-start(bf16[1024,128]{1,0:T(8,128)(2,1)} %slice.12), channel_id=1, source_target_pairs={{8,0},{16,8},{24,16},{9,1},{17,9},{25,17},{10,2},{18,10},{26,18},{... | collective-permute-start | bytes 786440 | tf_op jit(solution)/shard_map/ppermute | solution.py:212
  44.7 0.1 pad_add_fusion.place
  44.8 4.7 %collective-permute-done.1.refs_2_ = bf16[1024,128]{1,0:T(8,128)(2,1)S(1)} collective-permute-done((bf16[1024,128]{1,0:T(8,128)(2,1)S(1)}, bf16[1024,128]{1,0:T(8,128)(2,1)S(1)}, u32[]{:S(2)}, u32[]{:S(2)}) %collective-permute-start.1) | collective-permute-done | bytes 262176 | tf_op jit(solution)/shard_map/ppermute | solution.py:212
  49.5 4.2 %collective-permute-done.2.refs_3_ = bf16[1024,128]{1,0:T(8,128)(2,1)S(1)} collective-permute-done((bf16[1024,128]{1,0:T(8,128)(2,1)}, bf16[1024,128]{1,0:T(8,128)(2,1)S(1)}, u32[]{:S(2)}, u32[]{:S(2)}) %collective-permute-start.2) | collective-permute-done | bytes 262176 | tf_op jit(solution)/shard_map/ppermute | solution.py:212
  53.7 0.7 all-gather.3.cloned.1.call-done
  54.5 5.6 %shard_map.77 = f32[4096,128]{1,0:T(8,128)} custom-call(s32[3]{0:T(128)S(1)} %pad_add_fusion.place, bf16[8,2048,128]{2,1,0:T(8,128)(2,1)} %bitcast.15, bf16[2048,128]{1,0:T(8,128)(2,1)S(1)} %copy-done, bf16[2048,128]{1,0:T(8,128)(2,1)S(1)} %collective-permute-done.refs_1_, bf16[1024,128]{1,0:T(8,128)(2,1)S(1)} %collective-permute-done.1.refs_2_, ...), custom_call_target="tpu_custom_call" | custom-call | flops 2147483648 | bytes 8388608 | tf_op jit(solution)/shard_map/pallas_call | solution.py:64
  60.1 18.7 %all-to-all-done.offered_ref = bf16[16,272,128]{2,1,0:T(8,128)(2,1)S(1)} async-done(((bf16[16,272,128]{2,1,0:T(8,128)(2,1)}), bf16[16,272,128]{2,1,0:T(8,128)(2,1)S(1)}, u32[]{:S(2)}, u32[]{:S(2)}) %all-to-all-start) | async-done | bytes 1114144 | tf_op jit(solution)/shard_map/all_to_all | solution.py:204
  78.8 1.5 %shard_map.79 = (f32[16,128,128]{2,1,0:T(8,128)S(1)}, f32[16,128,128]{2,1,0:T(8,128)S(1)}) custom-call(s32[16,2]{1,0:T(8,128)S(1)} %bitcast.14, s32[1]{0:T(128)} %bitcast.6.core, bf16[16,272,128]{2,1,0:T(8,128)(2,1)S(1)} %all-to-all-done.offered_ref, bf16[8,128,128]{2,1,0:T(8,128)(2,1)S(1)} %bitcast.13), custom_call_target="tpu_custom_call" | custom-call | tf_op jit(solution)/shard_map/pallas_call | solution.py:152
  80.3 1.9 %collective-permute-start.4 = (f32[16,128,128]{2,1,0:T(8,128)S(1)}, f32[16,128,128]{2,1,0:T(8,128)S(1)}, u32[]{:S(2)}, u32[]{:S(2)}) collective-permute-start(f32[16,128,128]{2,1,0:T(8,128)S(1)} %get-tuple-element.9), channel_id=1, source_target_pairs={{0,1},{1,0},{2,3},{3,2},{4,5},{5,4},{6,7},{7,6},{8,9},{9,8},{10,11... | collective-permute-start | bytes 3145736 | tf_op jit(solution)/shard_map/ppermute | solution.py:231
  82.2 2.6 %collective-permute-done.4 = f32[16,128,128]{2,1,0:T(8,128)S(1)} collective-permute-done((f32[16,128,128]{2,1,0:T(8,128)S(1)}, f32[16,128,128]{2,1,0:T(8,128)S(1)}, u32[]{:S(2)}, u32[]{:S(2)}) %collective-permute-start.4) | collective-permute-done | bytes 1048608 | tf_op jit(solution)/shard_map/ppermute | solution.py:231
  84.8 0.1 add.10
  85.0 22.4 %all_to_all.15 = f32[16,128,128]{2,1,0:T(8,128)S(1)} all-to-all(f32[16,128,128]{2,1,0:T(8,128)S(1)} %add.10), channel_id=1, replica_groups={{0,2,4,6,8,10,12,14,16,18,20,22,24,26,28,30},{1,3,5,7,9,11,13,15,17,19,..., dimensions={0} | all-to-all | bytes 2097152 | tf_op jit(solution)/shard_map/all_to_all | solution.py:233
  107.4 0.1 reduce_sum.9
  107.4 21.4 %all_to_all.16 = f32[16,8,128]{2,1,0:T(8,128)} all-to-all(f32[16,8,128]{2,1,0:T(8,128)S(1)} %bitcast.16), channel_id=1, replica_groups=mesh['corpus'=16,'frow'=4,'fcol'=8] {'corpus'}, dimensions={0} | all-to-all | bytes 131072 | tf_op jit(solution)/shard_map/all_to_all | solution.py:237
  128.9 1.5 %shard_map.80 = f32[16,4,128]{2,1,0:T(4,128)} custom-call(s32[1,16]{1,0:T(1,128)} %get-tuple-element.6.places, s32[1,16]{1,0:T(1,128)} %trains.3, s32[1]{0:T(128)S(6)} %copy.13.count, f32[32,4,128]{2,1,0:T(4,128)} %bitcast.17, f32[16,128]{1,0:T(8,128)} %bitcast.19), custom_call_target="tpu_custom_call" | custom-call | tf_op jit(solution)/shard_map/pallas_call | solution.py:178
  130.4 4.0 %reduce-scatter.2.cloned.1.call-done = f32[256,128]{1,0:T(8,128)} async-done(((f32[4096,128]{1,0:T(8,128)}), f32[256,128]{1,0:T(8,128)}) %reduce-scatter.2.cloned.1.call-update) | async-done | bytes 131088 | tf_op jit(solution)/shard_map/reduce_scatter | solution.py:223
  (10 shorter events, 0.1 us)
Async XLA Ops:
  7.2 47.3 %all-gather.3.cloned.1.call-start = ((), (), s32[]{:S(2)}) async-start(), calls=%async_computation.5 | async-start | bytes 4718592 | tf_op jit(solution)/shard_map/all_gather | solution.py:207
  10.9 15.4 %copy-start = (bf16[2048,128]{1,0:T(8,128)(2,1)S(1)}, bf16[2048,128]{1,0:T(8,128)(2,1)}, u32[]{:S(2)}) copy-start(bf16[2048,128]{1,0:T(8,128)(2,1)} %refs_0_.1) | copy-start | bytes 1572868
  10.9 67.9 %all-to-all-start = ((bf16[16,272,128]{2,1,0:T(8,128)(2,1)}), bf16[16,272,128]{2,1,0:T(8,128)(2,1)S(1)}, u32[]{:S(2)}, u32[]{:S(2)}) async-start(bf16[16,272,128]{2,1,0:T(8,128)(2,1)} %get-tuple-element.7), calls=%async_computation.1 | async-start | bytes 2228224 | tf_op jit(solution)/shard_map/all_to_all | solution.py:204
  26.2 108.2 %reduce-scatter.2.cloned.1.call-start = ((), (), s32[]{:S(2)}) async-start(), calls=%async_computation.4 | async-start | bytes 2228224 | tf_op jit(solution)/shard_map/reduce_scatter | solution.py:223
  26.3 15.8 %collective-permute-start = (bf16[2048,128]{1,0:T(8,128)(2,1)S(1)}, bf16[2048,128]{1,0:T(8,128)(2,1)S(1)}, u32[]{:S(2)}, u32[]{:S(2)}) collective-permute-start(bf16[2048,128]{1,0:T(8,128)(2,1)S(1)} %copy-done), channel_id=1, source_target_pairs={{8,0},{16,8},{24,16},{9,1},{17,9},{25,17},{10,2},{18,10},{26,18},{... | collective-permute-start | bytes 1572872 | tf_op jit(solution)/shard_map/ppermute | solution.py:212
  28.7 20.8 %collective-permute-start.3 = (bf16[2048,128]{1,0:T(8,128)(2,1)S(1)}, bf16[2048,128]{1,0:T(8,128)(2,1)S(1)}, u32[]{:S(2)}, u32[]{:S(2)}) collective-permute-start(bf16[2048,128]{1,0:T(8,128)(2,1)S(1)} %copy-done), channel_id=1, source_target_pairs={{24,0},{25,1},{26,2},{27,3},{28,4},{29,5},{30,6},{31,7},{56,32},{5... | collective-permute-start | bytes 1572872 | tf_op jit(solution)/shard_map/ppermute | solution.py:212
  29.4 20.0 %collective-permute-start.1 = (bf16[1024,128]{1,0:T(8,128)(2,1)S(1)}, bf16[1024,128]{1,0:T(8,128)(2,1)S(1)}, u32[]{:S(2)}, u32[]{:S(2)}) collective-permute-start(bf16[1024,128]{1,0:T(8,128)(2,1)S(1)} %slice.9), channel_id=1, source_target_pairs={{16,0},{24,8},{17,1},{25,9},{18,2},{26,10},{19,3},{27,11},{20,4},{... | collective-permute-start | bytes 786440 | tf_op jit(solution)/shard_map/ppermute | solution.py:212
  42.8 10.9 %collective-permute-start.2 = (bf16[1024,128]{1,0:T(8,128)(2,1)}, bf16[1024,128]{1,0:T(8,128)(2,1)S(1)}, u32[]{:S(2)}, u32[]{:S(2)}) collective-permute-start(bf16[1024,128]{1,0:T(8,128)(2,1)} %slice.12), channel_id=1, source_target_pairs={{8,0},{16,8},{24,16},{9,1},{17,9},{25,17},{10,2},{18,10},{26,18},{... | collective-permute-start | bytes 786440 | tf_op jit(solution)/shard_map/ppermute | solution.py:212
  60.1 18.7 %copy-start.1 = (bf16[1024,128]{1,0:T(8,128)(2,1)S(1)}, bf16[1024,128]{1,0:T(8,128)(2,1)}, u32[]{:S(2)}) copy-start(bf16[1024,128]{1,0:T(8,128)(2,1)} %param.7) | copy-start | bytes 786436
  80.3 4.6 %collective-permute-start.4 = (f32[16,128,128]{2,1,0:T(8,128)S(1)}, f32[16,128,128]{2,1,0:T(8,128)S(1)}, u32[]{:S(2)}, u32[]{:S(2)}) collective-permute-start(f32[16,128,128]{2,1,0:T(8,128)S(1)} %get-tuple-element.9), channel_id=1, source_target_pairs={{0,1},{1,0},{2,3},{3,2},{4,5},{5,4},{6,7},{7,6},{8,9},{9,8},{10,11... | collective-permute-start | bytes 3145736 | tf_op jit(solution)/shard_map/ppermute | solution.py:231
Sparse Core Ops, SparseCore 0:
  10.1 44.2 all-gather.2
  60.2 74.1 reduce-scatter.1

commit v7 on v6

--- a/solution.py
+++ b/solution.py
@@ -101,11 +101,13 @@
         id_of[place] = lax.bitwise_and(test, held - 1)
         places[0, slot] = jnp.where(slot < live, place, 0)
     lane = lax.broadcasted_iota(jnp.int32, (ID_ROWS, TB), 1)
+    blocks = [block_of[at] for at in range(holders * CAP)]
+    asked = [id_of[at] for at in range(holders * CAP)]
     for h in range(holders):
         ids = jnp.zeros((ID_ROWS, TB), jnp.int32)
         for r in range(CAP):
-            out_ref[h, r * TB:(r + 1) * TB, :] = trains_ref[block_of[h * CAP + r]]
-            ids = jnp.where(lane == r, id_of[h * CAP + r], ids)
+            out_ref[h, r * TB:(r + 1) * TB, :] = trains_ref[blocks[h * CAP + r]]
+            ids = jnp.where(lane == r, asked[h * CAP + r], ids)
         out_ref[h, CAP * TB:, :] = ids.astype(jnp.float32).astype(out_ref.dtype)
 
 
@@ -180,6 +182,7 @@
         out_shape=jax.ShapeDtypeStruct((PAIRS,) + scores.shape[1:], jnp.float32),
         in_specs=[smem] * 3 + [vmem] * 2,
         out_specs=vmem,
+        compiler_params=pltpu.CompilerParams(vmem_limit_bytes=8 * 1024 * 1024),
     )(places, pair_trains, pair_counts, scores, weights)
 
 

time: 142 us -> 142 us (level)
  the two profiles are of different devices: /device:TPU:2 before, /device:TPU:22 now
where the time goes in v7:
time: 142 us; the launch traced here: 141 us
  waiting for transfers between devices  45 us (32%)
  blocking collectives  41.7 us (29%)
  starting transfers between devices  28.2 us (20%)
  between operations  14.8 us (10%)
  Pallas kernels  10.6 us (7%)
    all_to_all x1, blocking collectives, shards(): lax.all_to_all(summed.reshape(corpus_size, -1, TB), 'corpus', 0, 0, tiled...  21.2 us
    all_to_all x1, blocking collectives, shards(): lax.all_to_all(partials, ('frow', 'fcol'), 0, 0, axis_index_groups=same_c...  20.5 us
    all_to_all x1, waiting for transfers between devices, shards(): offered = lax.all_to_all(offered, 'corpus', 0, 0, tiled=True)  20.2 us
    all_to_all x1, starting transfers between devices, shards(): offered = lax.all_to_all(offered, 'corpus', 0, 0, tiled=True)  15.3 us
    ppermute x4, waiting for transfers between devices, down(): return lax.ppermute(rows, 'frow', pairs)  13.2 us
    ppermute x4, starting transfers between devices, down(): return lax.ppermute(rows, 'frow', pairs)  10.9 us
    reduce_scatter x1, waiting for transfers between devices, shards(): lax.psum_scatter(tile, 'corpus', scatter_dimension=0, tiled=True)  6.57 us
    pallas_call x1, Pallas kernels, gram_tile(): pl.pallas_call(functools.partial(gram_kernel, scale, x_size, cuts), out_s...  5.61 us
  transfers between devices with their start and end apart: 8, of which 7 were waited for; matrix products, arithmetic and copies ran while one was open for 1% of the time, Pallas kernels for 7%

profile of v7, /device:TPU:22, one launch (start us, length us, event | category | flops | bytes accessed | tf_op | source)
XLA Modules:
  0.0 141.4 jit_solution(2665351857340030143)
XLA Ops:
  7.2 0.7 all-gather.3.cloned.1.call-update
  8.5 2.3 %shard_map.78 = (bf16[16,272,128]{2,1,0:T(8,128)(2,1)}, s32[1,16]{1,0:T(1,128)}) custom-call(s32[1,16]{1,0:T(1,128)} %tests.1, s32[1,16]{1,0:T(1,128)} %trains.3, s32[1]{0:T(128)S(6)} %copy.13.count, bf16[16,128,128]{2,1,0:T(8,128)(2,1)} %bitcast.12), custom_call_target="tpu_custom_call" | custom-call | tf_op jit(solution)/shard_map/pallas_call | solution.py:117
  10.8 15.3 %all-to-all-start = ((bf16[16,272,128]{2,1,0:T(8,128)(2,1)}), bf16[16,272,128]{2,1,0:T(8,128)(2,1)S(1)}, u32[]{:S(2)}, u32[]{:S(2)}) async-start(bf16[16,272,128]{2,1,0:T(8,128)(2,1)} %get-tuple-element.7), calls=%async_computation.1 | async-start | bytes 2228224 | tf_op jit(solution)/shard_map/all_to_all | solution.py:207
  26.2 2.8 %collective-permute-start = (bf16[2048,128]{1,0:T(8,128)(2,1)S(1)}, bf16[2048,128]{1,0:T(8,128)(2,1)S(1)}, u32[]{:S(2)}, u32[]{:S(2)}) collective-permute-start(bf16[2048,128]{1,0:T(8,128)(2,1)S(1)} %copy-done), channel_id=1, source_target_pairs={{8,0},{16,8},{24,16},{9,1},{17,9},{25,17},{10,2},{18,10},{26,18},{... | collective-permute-start | bytes 1572872 | tf_op jit(solution)/shard_map/ppermute | solution.py:215
  29.0 1.3 collective-permute-start.3
  30.4 2.4 %collective-permute-start.1 = (bf16[1024,128]{1,0:T(8,128)(2,1)S(1)}, bf16[1024,128]{1,0:T(8,128)(2,1)S(1)}, u32[]{:S(2)}, u32[]{:S(2)}) collective-permute-start(bf16[1024,128]{1,0:T(8,128)(2,1)S(1)} %slice.9), channel_id=1, source_target_pairs={{16,0},{24,8},{17,1},{25,9},{18,2},{26,10},{19,3},{27,11},{20,4},{... | collective-permute-start | bytes 786440 | tf_op jit(solution)/shard_map/ppermute | solution.py:215
  32.8 8.6 %collective-permute-done.refs_1_ = bf16[2048,128]{1,0:T(8,128)(2,1)S(1)} collective-permute-done((bf16[2048,128]{1,0:T(8,128)(2,1)S(1)}, bf16[2048,128]{1,0:T(8,128)(2,1)S(1)}, u32[]{:S(2)}, u32[]{:S(2)}) %collective-permute-start) | collective-permute-done | bytes 524320 | tf_op jit(solution)/shard_map/ppermute | solution.py:215
  41.3 0.7 slice.12
  42.1 4.4 %collective-permute-start.2 = (bf16[1024,128]{1,0:T(8,128)(2,1)}, bf16[1024,128]{1,0:T(8,128)(2,1)S(1)}, u32[]{:S(2)}, u32[]{:S(2)}) collective-permute-start(bf16[1024,128]{1,0:T(8,128)(2,1)} %slice.12), channel_id=1, source_target_pairs={{8,0},{16,8},{24,16},{9,1},{17,9},{25,17},{10,2},{18,10},{26,18},{... | collective-permute-start | bytes 786440 | tf_op jit(solution)/shard_map/ppermute | solution.py:215
  46.5 0.1 pad_add_fusion.place
  46.5 0.3 collective-permute-done.1.refs_2_
  46.9 4.3 %collective-permute-done.2.refs_3_ = bf16[1024,128]{1,0:T(8,128)(2,1)S(1)} collective-permute-done((bf16[1024,128]{1,0:T(8,128)(2,1)}, bf16[1024,128]{1,0:T(8,128)(2,1)S(1)}, u32[]{:S(2)}, u32[]{:S(2)}) %collective-permute-start.2) | collective-permute-done | bytes 262176 | tf_op jit(solution)/shard_map/ppermute | solution.py:215
  51.2 1.7 %all-gather.3.cloned.1.call-done = bf16[16384,128]{1,0:T(8,128)(2,1)} async-done(((bf16[2048,128]{1,0:T(8,128)(2,1)}), bf16[16384,128]{1,0:T(8,128)(2,1)}) %all-gather.3.cloned.1.call-update) | async-done | bytes 4194320 | tf_op jit(solution)/shard_map/all_gather | solution.py:210
  52.9 5.6 %shard_map.77 = f32[4096,128]{1,0:T(8,128)} custom-call(s32[3]{0:T(128)S(1)} %pad_add_fusion.place, bf16[8,2048,128]{2,1,0:T(8,128)(2,1)} %bitcast.17, bf16[2048,128]{1,0:T(8,128)(2,1)S(1)} %copy-done, bf16[2048,128]{1,0:T(8,128)(2,1)S(1)} %collective-permute-done.refs_1_, bf16[1024,128]{1,0:T(8,128)(2,1)S(1)} %collective-permute-done.1.refs_2_, ...), custom_call_target="tpu_custom_call" | custom-call | flops 2147483648 | bytes 8388608 | tf_op jit(solution)/shard_map/pallas_call | solution.py:64
  58.6 20.2 %all-to-all-done.offered_ref = bf16[16,272,128]{2,1,0:T(8,128)(2,1)S(1)} async-done(((bf16[16,272,128]{2,1,0:T(8,128)(2,1)}), bf16[16,272,128]{2,1,0:T(8,128)(2,1)S(1)}, u32[]{:S(2)}, u32[]{:S(2)}) %all-to-all-start) | async-done | bytes 1114144 | tf_op jit(solution)/shard_map/all_to_all | solution.py:207
  78.8 1.5 %shard_map.79 = (f32[16,128,128]{2,1,0:T(8,128)S(1)}, f32[16,128,128]{2,1,0:T(8,128)S(1)}) custom-call(s32[16,2]{1,0:T(8,128)S(1)} %bitcast.15, s32[1]{0:T(128)} %bitcast.6.core, bf16[16,272,128]{2,1,0:T(8,128)(2,1)S(1)} %all-to-all-done.offered_ref, bf16[8,128,128]{2,1,0:T(8,128)(2,1)S(1)} %bitcast.13), custom_call_target="tpu_custom_call" | custom-call | tf_op jit(solution)/shard_map/pallas_call | solution.py:154
  80.3 1.9 %collective-permute-start.4 = (f32[16,128,128]{2,1,0:T(8,128)S(1)}, f32[16,128,128]{2,1,0:T(8,128)S(1)}, u32[]{:S(2)}, u32[]{:S(2)}) collective-permute-start(f32[16,128,128]{2,1,0:T(8,128)S(1)} %get-tuple-element.9), channel_id=1, source_target_pairs={{0,1},{1,0},{2,3},{3,2},{4,5},{5,4},{6,7},{7,6},{8,9},{9,8},{10,11... | collective-permute-start | bytes 3145736 | tf_op jit(solution)/shard_map/ppermute | solution.py:234
  82.2 2.6 %collective-permute-done.4 = f32[16,128,128]{2,1,0:T(8,128)S(1)} collective-permute-done((f32[16,128,128]{2,1,0:T(8,128)S(1)}, f32[16,128,128]{2,1,0:T(8,128)S(1)}, u32[]{:S(2)}, u32[]{:S(2)}) %collective-permute-start.4) | collective-permute-done | bytes 1048608 | tf_op jit(solution)/shard_map/ppermute | solution.py:234
  84.8 0.1 add.10
  85.0 20.5 %all_to_all.15 = f32[16,128,128]{2,1,0:T(8,128)S(1)} all-to-all(f32[16,128,128]{2,1,0:T(8,128)S(1)} %add.10), channel_id=1, replica_groups={{0,2,4,6,8,10,12,14,16,18,20,22,24,26,28,30},{1,3,5,7,9,11,13,15,17,19,..., dimensions={0} | all-to-all | bytes 2097152 | tf_op jit(solution)/shard_map/all_to_all | solution.py:236
  105.4 0.1 reduce_sum.9
  105.5 21.2 %all_to_all.16 = f32[16,8,128]{2,1,0:T(8,128)S(1)} all-to-all(f32[16,8,128]{2,1,0:T(8,128)S(1)} %bitcast.18), channel_id=1, replica_groups=mesh['corpus'=16,'frow'=4,'fcol'=8] {'corpus'}, dimensions={0} | all-to-all | bytes 131072 | tf_op jit(solution)/shard_map/all_to_all | solution.py:240
  126.7 1.2 shard_map.80
  127.9 6.6 %reduce-scatter.2.cloned.1.call-done = f32[256,128]{1,0:T(8,128)} async-done(((f32[4096,128]{1,0:T(8,128)}), f32[256,128]{1,0:T(8,128)}) %reduce-scatter.2.cloned.1.call-update) | async-done | bytes 131088 | tf_op jit(solution)/shard_map/reduce_scatter | solution.py:226
  (16 shorter events, 0.1 us)
Async XLA Ops:
  7.2 45.7 %all-gather.3.cloned.1.call-start = ((), (), s32[]{:S(2)}) async-start(), calls=%async_computation.5 | async-start | bytes 4718592 | tf_op jit(solution)/shard_map/all_gather | solution.py:210
  10.8 15.4 %copy-start = (bf16[2048,128]{1,0:T(8,128)(2,1)S(1)}, bf16[2048,128]{1,0:T(8,128)(2,1)}, u32[]{:S(2)}) copy-start(bf16[2048,128]{1,0:T(8,128)(2,1)} %refs_0_.1) | copy-start | bytes 1572868
  10.8 67.9 %all-to-all-start = ((bf16[16,272,128]{2,1,0:T(8,128)(2,1)}), bf16[16,272,128]{2,1,0:T(8,128)(2,1)S(1)}, u32[]{:S(2)}, u32[]{:S(2)}) async-start(bf16[16,272,128]{2,1,0:T(8,128)(2,1)} %get-tuple-element.7), calls=%async_computation.1 | async-start | bytes 2228224 | tf_op jit(solution)/shard_map/all_to_all | solution.py:207
  26.2 108.3 %reduce-scatter.2.cloned.1.call-start = ((), (), s32[]{:S(2)}) async-start(), calls=%async_computation.4 | async-start | bytes 2228224 | tf_op jit(solution)/shard_map/reduce_scatter | solution.py:226
  26.2 15.1 %collective-permute-start = (bf16[2048,128]{1,0:T(8,128)(2,1)S(1)}, bf16[2048,128]{1,0:T(8,128)(2,1)S(1)}, u32[]{:S(2)}, u32[]{:S(2)}) collective-permute-start(bf16[2048,128]{1,0:T(8,128)(2,1)S(1)} %copy-done), channel_id=1, source_target_pairs={{8,0},{16,8},{24,16},{9,1},{17,9},{25,17},{10,2},{18,10},{26,18},{... | collective-permute-start | bytes 1572872 | tf_op jit(solution)/shard_map/ppermute | solution.py:215
  29.0 17.9 %collective-permute-start.3 = (bf16[2048,128]{1,0:T(8,128)(2,1)S(1)}, bf16[2048,128]{1,0:T(8,128)(2,1)S(1)}, u32[]{:S(2)}, u32[]{:S(2)}) collective-permute-start(bf16[2048,128]{1,0:T(8,128)(2,1)S(1)} %copy-done), channel_id=1, source_target_pairs={{24,0},{25,1},{26,2},{27,3},{28,4},{29,5},{30,6},{31,7},{56,32},{5... | collective-permute-start | bytes 1572872 | tf_op jit(solution)/shard_map/ppermute | solution.py:215
  30.4 16.5 %collective-permute-start.1 = (bf16[1024,128]{1,0:T(8,128)(2,1)S(1)}, bf16[1024,128]{1,0:T(8,128)(2,1)S(1)}, u32[]{:S(2)}, u32[]{:S(2)}) collective-permute-start(bf16[1024,128]{1,0:T(8,128)(2,1)S(1)} %slice.9), channel_id=1, source_target_pairs={{16,0},{24,8},{17,1},{25,9},{18,2},{26,10},{19,3},{27,11},{20,4},{... | collective-permute-start | bytes 786440 | tf_op jit(solution)/shard_map/ppermute | solution.py:215
  42.1 9.1 %collective-permute-start.2 = (bf16[1024,128]{1,0:T(8,128)(2,1)}, bf16[1024,128]{1,0:T(8,128)(2,1)S(1)}, u32[]{:S(2)}, u32[]{:S(2)}) collective-permute-start(bf16[1024,128]{1,0:T(8,128)(2,1)} %slice.12), channel_id=1, source_target_pairs={{8,0},{16,8},{24,16},{9,1},{17,9},{25,17},{10,2},{18,10},{26,18},{... | collective-permute-start | bytes 786440 | tf_op jit(solution)/shard_map/ppermute | solution.py:215
  58.5 20.2 %copy-start.1 = (bf16[1024,128]{1,0:T(8,128)(2,1)S(1)}, bf16[1024,128]{1,0:T(8,128)(2,1)}, u32[]{:S(2)}) copy-start(bf16[1024,128]{1,0:T(8,128)(2,1)} %param.7) | copy-start | bytes 786436
  80.3 4.6 %collective-permute-start.4 = (f32[16,128,128]{2,1,0:T(8,128)S(1)}, f32[16,128,128]{2,1,0:T(8,128)S(1)}, u32[]{:S(2)}, u32[]{:S(2)}) collective-permute-start(f32[16,128,128]{2,1,0:T(8,128)S(1)} %get-tuple-element.9), channel_id=1, source_target_pairs={{0,1},{1,0},{2,3},{3,2},{4,5},{5,4},{6,7},{7,6},{8,9},{9,8},{10,11... | collective-permute-start | bytes 3145736 | tf_op jit(solution)/shard_map/ppermute | solution.py:234
  105.4 21.3 %copy-start.2 = (f32[2048]{0:T(1024)S(1)}, f32[2048]{0:T(1024)}, u32[]{:S(2)}) copy-start(f32[2048]{0:T(1024)} %param.8) | copy-start | bytes 24580
  105.4 21.3 %copy-start.3 = (s32[1,16]{1,0:T(1,128)S(1)}, s32[1,16]{1,0:T(1,128)}, u32[]{:S(2)}) copy-start(s32[1,16]{1,0:T(1,128)} %trains.3) | copy-start | bytes 196
  105.4 21.3 %copy-start.4 = (s32[1,16]{1,0:T(1,128)S(1)}, s32[1,16]{1,0:T(1,128)}, u32[]{:S(2)}) copy-start(s32[1,16]{1,0:T(1,128)} %get-tuple-element.6.places) | copy-start | bytes 196
Sparse Core Ops, SparseCore 0:
  10.1 42.6 all-gather.2
  58.7 75.8 reduce-scatter.1
